TPU v7x, 512 devices: a whole 4x8x8 slice. The times are simulated.
512 devices in a mesh: row: 64 (over z, x, core), grp: 8 (over y).
Axes of the slice: x: 4, y: 8, z: 8, core: 2. Of those that a mesh axis runs over, the one named last changes fastest.
Arguments:
- a_blocks: bfloat16 [4096, 64, 1024], P(('row', 'grp')), may hold values from -0.75 to 0.75
- p_blocks: bfloat16 [4096, 64, 128], P(('row', 'grp')), may hold values from -0.75 to 0.75
- a_cols: int32 [4096, 16], P(('row', 'grp')), may hold values from 0 to 455
- a_live: int32 [512], P(('row', 'grp')), may hold values from 2 to 8, as said below
- group_need: int32 [512, 8, 8], P(('row', 'grp')), may hold values from 0 to 7
- row_send: int32 [512, 64, 6], P(('row', 'grp')), may hold values from 0 to 7
Outputs:
- coarse: bfloat16 [64, 64, 128, 128], P('row', 'grp')
Inputs may be any that keep to these rules, and one draw needn't show every extreme that they name: `a_live`: some device has all 8 rows active; the others between a quarter and all of them.
All inputs are finite; a program needn't handle non-finite values.
Results may differ from a plain program's by a relative error of at most 0.015.
Values may be sent and summed in bfloat16 or wider, within the bound.
No kernel may reach another device: no remote copies, remote signals or barrier semaphores. Data moves between devices by JAX's collectives and lax.ppermute only.
A program may use at most 128 MiB of HBM per device.

v0:
```python
import jax
import jax.numpy as jnp
from jax import lax
from jax.sharding import PartitionSpec as P


def shards(a_blocks, p_blocks, a_cols, a_live, group_need, row_send):
    tile_rows = a_blocks.shape[0]
    block_size = p_blocks.shape[1]
    coarse_width = p_blocks.shape[2]
    slot_count = a_blocks.shape[2] // block_size
    row_count = lax.axis_size("row")
    group_size = lax.axis_size("grp")
    my_group = lax.axis_index("row")
    needed = group_need[0]
    panel_rows = lax.all_gather(p_blocks, "grp", axis=0, tiled=True)
    offsets = jnp.arange(group_size, dtype=jnp.int32)[:, None] * tile_rows
    neighbours = panel_rows[(offsets + needed).reshape(-1)]
    outgoing = p_blocks[row_send[0].reshape(-1)].reshape(row_count, -1, block_size, coarse_width)
    remote = lax.all_to_all(outgoing, "row", split_axis=0, concat_axis=0, tiled=True).reshape(
        -1, block_size, coarse_width
    )
    ghost_each = remote.shape[0] // row_count
    near_count = tile_rows + neighbours.shape[0]
    lookup_table = jnp.concatenate([p_blocks, neighbours, remote], 0)
    panels = jnp.where(a_cols < near_count, my_group, (a_cols - near_count) // ghost_each)
    step_rows = min(8, tile_rows)
    live_rows = a_live[0]

    def accumulate(turn_index, running):
        first_row = turn_index * step_rows
        left_side = jnp.einsum(
            "rkc,rkn->rcn", p_blocks, a_blocks, preferred_element_type=jnp.float32
        ).astype(jnp.bfloat16)
        left_side = left_side.reshape(step_rows, coarse_width, slot_count, block_size)
        right_side = lookup_table[a_cols]
        products = jnp.einsum(
            "rcsk,rskq->rscq", left_side, right_side, preferred_element_type=jnp.float32
        )
        active = (first_row + jnp.arange(step_rows, dtype=jnp.int32) < live_rows).astype(
            jnp.float32
        )
        products = products * active[:, None, None, None]
        return running.at[panels.reshape(-1)].add(products.reshape(-1, coarse_width, coarse_width))

    turn_count = (live_rows + step_rows - 1) // step_rows
    running = lax.fori_loop(
        0, turn_count, accumulate, jnp.zeros((row_count, coarse_width, coarse_width), jnp.float32)
    )
    summed = lax.psum_scatter(running.astype(jnp.bfloat16), "grp", scatter_dimension=0, tiled=True)
    return summed[None]


def solution(mesh):
    placed = (
        P(("row", "grp"), None, None),
        P(("row", "grp"), None, None),
        P(("row", "grp"), None),
        P(("row", "grp")),
        P(("row", "grp"), None, None),
        P(("row", "grp"), None, None),
    )
    return jax.shard_map(
        shards, mesh=mesh, in_specs=placed, out_specs=P("row", "grp", None, None), check_vma=False
    )
```

profile of v0, /device:TPU:1, one launch (start us, length us, event | category | flops | bytes accessed | tf_op | source)
XLA Modules:
  0.0 270.3 jit_solution(17425481352406405665)
XLA Ops:
  6.5 0.0 copy-start
  6.5 0.9 copy.11
  7.4 0.1 reshape_squeeze.3
  7.6 4.9 %gather_fusion.1 = bf16[384,64,128]{2,1,0:T(8,128)(2,1)} fusion(bf16[8,64,128]{2,1,0:T(8,128)(2,1)} %param.9, s32[1024]{0:T(1024)S(1)} %pad_clamp_fusion.1), kind=kCustom, calls=%fused_computation.1 | custom fusion | bytes 12584448 | tf_op jit(solution)/shard_map/gather | solution.py:19
  12.5 0.0 copy-start.4
  12.5 0.0 copy-start.3
  12.5 0.0 copy-start.1
  12.5 15.1 %all-to-all-start = ((bf16[64,6,64,128]{3,2,1,0:T(8,128)(2,1)}), bf16[64,6,64,128]{3,2,1,0:T(8,128)(2,1)}, u32[]{:S(2)}, u32[]{:S(2)}) async-start(bf16[64,6,64,128]{3,2,1,0:T(8,128)(2,1)} %bitcast.23), calls=%async_computation | async-start | bytes 12582912 | tf_op jit(solution)/shard_map/all_to_all | solution.py:20
  27.7 0.0 all-gather.2.cloned.1.call-start
  27.7 0.7 all-gather.2.cloned.1.call-update
  28.4 0.0 reduce-scatter.2.cloned.1.call-start
  29.1 0.0 copy-done.4
  29.1 0.1 squeeze.7
  29.2 0.1 add.91
  29.3 0.1 add.92
  29.4 0.0 copy-done.3
  29.4 0.0 copy-start.2
  29.4 0.1 reshape.147
  29.5 0.1 reshape.164
  29.6 0.0 copy-done
  29.6 0.0 copy-done.1
  29.6 0.8 convolution_convert_fusion
  30.3 2.4 copy.10
  32.7 36.0 %all-gather.2.cloned.1.call-done = bf16[64,64,128]{2,1,0:T(8,128)(2,1)} async-done(((bf16[8,64,128]{2,1,0:T(8,128)(2,1)}), bf16[64,64,128]{2,1,0:T(8,128)(2,1)}) %all-gather.2.cloned.1.call-update) | async-done | bytes 1048592 | tf_op jit(solution)/shard_map/all_gather | solution.py:16
  68.7 2.0 gather_fusion
  70.7 95.5 %all-to-all-done = bf16[64,6,64,128]{3,2,1,0:T(8,128)(2,1)} async-done(((bf16[64,6,64,128]{3,2,1,0:T(8,128)(2,1)}), bf16[64,6,64,128]{3,2,1,0:T(8,128)(2,1)}, u32[]{:S(2)}, u32[]{:S(2)}) %all-to-all-start) | async-done | bytes 6291488 | tf_op jit(solution)/shard_map/all_to_all | solution.py:20
  166.2 6.5 %pad_maximum_fusion = bf16[456,64,128]{2,1,0:T(8,128)(2,1)} fusion(bf16[384,64,128]{2,1,0:T(8,128)(2,1)} %bitcast.6, bf16[64,64,128]{2,1,0:T(8,128)(2,1)S(1)} %gather_fusion, bf16[8,64,128]{2,1,0:T(8,128)(2,1)S(1)} %copy-done.1), kind=kLoop, calls=%fused_computation.8 | loop fusion | flops 7471104 | bytes 14942208 | tf_op jit(solution)/shard_map/concatenate | solution.py:25
  172.7 0.0 copy-done.2
  172.7 4.1 %gather_fusion.2 = bf16[128,64,128]{2,1,0:T(8,128)(2,1)S(1)} fusion(bf16[456,64,128]{2,1,0:T(8,128)(2,1)} %pad_maximum_fusion, s32[1024]{0:T(1024)S(1)} %pad_clamp_fusion), kind=kCustom, calls=%fused_computation.2 | custom fusion | bytes 4194816 | tf_op jit(solution)/shard_map/while/body/gather | solution.py:36
  176.8 6.1 %fusion.5 = f32[8,16,128,128]{3,2,1,0:T(8,128)} fusion(bf16[8,128,16,64]{1,3,2,0:T(8,128)(2,1)} %bitcast.25, bf16[8,16,64,128]{3,2,1,0:T(8,128)(2,1)S(1)} %bitcast.24), kind=kOutput, calls=%fused_computation.24 | convolution fusion | flops 268435456 | bytes 12582912 | tf_op jit(solution)/shard_map/while/body/rcsk,rskq->rscq/dot_general | solution.py:37
  182.9 2.5 broadcast_in_dim.8
  185.4 34.5 %while.13 = (s32[]{:T(128)}, f32[64,128,128]{2,1,0:T(8,128)}, s32[]{:T(128)}, s32[8,16]{1,0:T(8,128)}, f32[8,16,128,128]{3,2,1,0:T(8,128)}, /*index=5*/s32[]{:T(128)}, s32[128,1]{0,1:T(1,128)S(1)}, s32[]{:T(128)}, s32[]{:T(128)}) while((s32[]{:T(128)}, f32[64,128,128]{2,1,0:T(8,128)}, s32[]{:T(128)}, s32[8,16]{1,0:T(8,128)}, ...), condition=%wide.wide.region_2.3_spmd, body=%wide.wide.region_0.2_spmd.sunk | while | flops 4194715 | bytes 41946800 | solution.py:47
  185.4 0.6 compare_convert_fusion.3
  186.0 0.1 mul.47
  186.1 0.1 mul.48
  186.2 7.2 %bitcast_multiply_fusion.3 = f32[128,128,128]{2,1,0:T(8,128)} fusion(f32[8,16,128,128]{3,2,1,0:T(8,128)} %get-tuple-element.211, f32[128]{0:T(128)S(1)} %mul.48), kind=kLoop, calls=%fused_computation.4.clone.clone.1 | loop fusion | flops 2097152 | bytes 16777728 | tf_op jit(solution)/shard_map/while/body/mul | solution.py:43
  193.4 26.5 %scatter_fusion = f32[64,128,128]{2,1,0:T(8,128)} fusion(f32[64,128,128]{2,1,0:T(8,128)} %get-tuple-element.199, s32[128]{0:T(128)S(1)} %fusion.12, f32[128,128,128]{2,1,0:T(8,128)} %bitcast_multiply_fusion.3), kind=kCustom, calls=%fused_computation.3.clone.clone.1 | custom fusion | flops 2097152 | bytes 25166336 | tf_op jit(solution)/shard_map/while/body/scatter-add | solution.py:44
  219.9 3.9 %convert_element_type.18 = bf16[64,128,128]{2,1,0:T(8,128)(2,1)} convert(f32[64,128,128]{2,1,0:T(8,128)} %get-tuple-element.105) | non-fusion elementwise | flops 1048576 | bytes 6291456 | tf_op jit(solution)/shard_map/convert_element_type | solution.py:50
  223.8 0.0 reduce-scatter.2.cloned.1.call-update
  223.8 39.7 %reduce-scatter.2.cloned.1.call-done = bf16[8,128,128]{2,1,0:T(8,128)(2,1)} async-done(((bf16[64,128,128]{2,1,0:T(8,128)(2,1)}), bf16[8,128,128]{2,1,0:T(8,128)(2,1)}) %reduce-scatter.2.cloned.1.call-update) | async-done | bytes 262160 | tf_op jit(solution)/shard_map/reduce_scatter | solution.py:50
  (8 shorter events, 0.1 us)
Async XLA Ops:
  6.5 23.0 %copy-start = (bf16[8,64,1024]{2,1,0:T(8,128)(2,1)S(1)}, bf16[8,64,1024]{2,1,0:T(8,128)(2,1)}, u32[]{:S(2)}) copy-start(bf16[8,64,1024]{2,1,0:T(8,128)(2,1)} %param.8) | copy-start | bytes 3145732
  12.5 16.6 %copy-start.4 = (s32[1,8,8]{2,1,0:T(8,128)S(1)}, s32[1,8,8]{2,1,0:T(8,128)}, u32[]{:S(2)}) copy-start(s32[1,8,8]{2,1,0:T(8,128)} %param.12) | copy-start | bytes 772
  12.5 16.8 %copy-start.3 = (s32[8,16]{1,0:T(8,128)S(1)}, s32[8,16]{1,0:T(8,128)}, u32[]{:S(2)}) copy-start(s32[8,16]{1,0:T(8,128)} %param.10) | copy-start | bytes 1540
  12.5 17.0 %copy-start.1 = (bf16[8,64,128]{2,1,0:T(8,128)(2,1)S(1)}, bf16[8,64,128]{2,1,0:T(8,128)(2,1)}, u32[]{:S(2)}) copy-start(bf16[8,64,128]{2,1,0:T(8,128)(2,1)} %param.9) | copy-start | bytes 393220
  12.5 153.7 %all-to-all-start = ((bf16[64,6,64,128]{3,2,1,0:T(8,128)(2,1)}), bf16[64,6,64,128]{3,2,1,0:T(8,128)(2,1)}, u32[]{:S(2)}, u32[]{:S(2)}) async-start(bf16[64,6,64,128]{3,2,1,0:T(8,128)(2,1)} %bitcast.23), calls=%async_computation | async-start | bytes 12582912 | tf_op jit(solution)/shard_map/all_to_all | solution.py:20
  27.7 41.0 %all-gather.2.cloned.1.call-start = ((), (), s32[]{:S(2)}) async-start(), calls=%async_computation.2 | async-start | bytes 1179648 | tf_op jit(solution)/shard_map/all_gather | solution.py:16
  28.4 235.1 %reduce-scatter.2.cloned.1.call-start = ((), (), s32[]{:S(2)}) async-start(), calls=%async_computation.3 | async-start | bytes 2359296 | tf_op jit(solution)/shard_map/reduce_scatter | solution.py:50
  29.4 143.3 %copy-start.2 = (s32[8,16]{1,0:T(8,128)}, s32[8,16]{1,0:T(8,128)S(1)}, u32[]{:S(2)}) copy-start(s32[8,16]{1,0:T(8,128)S(1)} %get-tuple-element.192) | copy-start | bytes 1540
Sparse Core Ops, SparseCore 0:
  30.6 38.0 all-gather.1
  223.9 39.4 reduce-scatter.1
where the time goes:
time: 274 us; the launch traced here: 270 us
  waiting for transfers between devices  172 us (63%)
  other arithmetic  44.8 us (16%)
  local copies, waits for them, and re-layouts  17.4 us (6%)
  starting transfers between devices  15.2 us (6%)
  between operations  14.2 us (5%)
  matrix products  6.9 us (3%)
    all_to_all x1, waiting for transfers between devices, shards(): lax.all_to_all(outgoing, 'row', split_axis=0, concat_axis=0, tiled=True)  95.5 us
    reduce_scatter x1, waiting for transfers between devices, shards(): lax.psum_scatter(running.astype(jnp.bfloat16), 'grp', scatter_dimension=0...  39.7 us
    all_gather x1, waiting for transfers between devices, shards(): panel_rows = lax.all_gather(p_blocks, 'grp', axis=0, tiled=True)  36 us
    scatter-add x1, other arithmetic, accumulate(): running.at[panels.reshape(-1)]  26.5 us
    all_to_all x1, starting transfers between devices, shards(): lax.all_to_all(outgoing, 'row', split_axis=0, concat_axis=0, tiled=True)  15.1 us
    mul x1, other arithmetic, accumulate(): products = products * active[:, None, None, None]  7.22 us
    concatenate x1, other arithmetic, shards(): lookup_table = jnp.concatenate([p_blocks, neighbours, remote], 0)  6.49 us
    dot_general x1, matrix products, accumulate(): jnp.einsum('rcsk,rskq->rscq', left_side, right_side, preferred_element_ty...  6.15 us
  transfers between devices with their start and end apart: 3, of which 3 were waited for; matrix products, arithmetic and copies ran while one was open for 2% of the time, Pallas kernels for 0%

commit v1 on v0

v1 whole, which is shorter than its diff:
```python
import functools

import jax
import jax.numpy as jnp
from jax import lax
from jax.experimental import pallas as pl
from jax.experimental.pallas import tpu as pltpu
from jax.sharding import Mesh, PartitionSpec as P

NZ, NX, NC, NY = 8, 4, 2, 8
RB, BS, CW, SA = 8, 64, 128, 16
GP = 6
NEAR = RB + NY * RB
SLOTS = RB * SA
PAD = 16
ROWS = RB * BS + PAD
UNROLL = 4
OFF = 255


def terms_kernel(place, code, sent, cols, need, a_ref, p_ref, near_ref, o_ref, left, acc, todo):
    turn = pl.program_id(0)
    my_z, my_x, my_c, live = place[0], place[1], place[2], place[3]

    for n in range(RB):
        rows = pl.ds(n * BS, BS)
        product = lax.dot_general(
            a_ref[0, rows, SA * BS :], a_ref[0, rows, : SA * BS], (((0,), (0,)), ((), ())),
            preferred_element_type=jnp.float32,
        ).astype(jnp.bfloat16)
        for pair in range(SA // 2):
            left[n * (SA // 2) + pair] = product[:, pair * CW : (pair + 1) * CW]
    acc[...] = jnp.zeros_like(acc)

    def add_terms(count, row_of):
        def body(step, unused):
            found = []
            for u in range(UNROLL):
                item = todo[step * UNROLL + u]
                slot = item & (SLOTS - 1)
                block = row_of(item)
                odd = (slot & 1) == 1
                zero = jnp.zeros_like(block)
                right = jnp.concatenate([jnp.where(odd, zero, block), jnp.where(odd, block, zero)], 0)
                found.append((item >> 16, jnp.dot(left[slot >> 1], right, preferred_element_type=jnp.float32)))
            for panel, term in found:
                acc[panel] += term
            return 0

        for u in range(UNROLL):
            todo[count + u] = (NC * NZ) << 16
        lax.fori_loop(0, (count + UNROLL - 1) // UNROLL, body, 0)

    def pick_far(slot, count):
        panel = code[turn, 0, slot]
        listed = code[turn, 1, slot]
        mine = (panel < NZ * NX * NC) & (((panel >> 1) & (NX - 1)) == my_x)
        source = jnp.where(mine, (panel & 1) * NZ + (panel >> 3), 0)
        row = sent[source, (turn * NC + my_c) * GP + listed]
        todo[count] = slot | (row << 8) | (source << 12) | (source << 16)
        return count + mine.astype(jnp.int32)

    far = lax.fori_loop(0, SLOTS, pick_far, 0, unroll=8)
    add_terms(far, lambda item: p_ref[(item >> 12) & 15, pl.ds(pl.multiple_of(((item >> 8) & 7) * BS, BS), BS), :])

    @pl.when(turn == my_x)
    def _():
        own = (my_c * NZ + my_z) << 16

        def pick_near(slot, count):
            entry = cols[slot]
            mine = (entry < NEAR) & ((slot >> 4) < live)
            listed = jnp.where(mine, jnp.maximum(entry - RB, 0), 0)
            member = jnp.where(entry < RB, place[4], listed >> 3)
            row = jnp.where(entry < RB, entry, need[listed])
            todo[count] = slot | (row << 8) | (jnp.where(mine, member, 0) << 12) | own
            return count + mine.astype(jnp.int32)

        close = lax.fori_loop(0, SLOTS, pick_near, 0, unroll=8)
        add_terms(close, lambda item: near_ref[(item >> 12) & 15, pl.ds(pl.multiple_of(((item >> 8) & 7) * BS, BS), BS), :])

    for source in range(NC * NZ):
        o_ref[0, source % NZ, source // NZ] = acc[source].astype(jnp.bfloat16)


def shards(a_blocks, p_blocks, a_cols, a_live, group_need, row_send):
    my_z, my_x, my_c, my_y = (lax.axis_index(axis) for axis in ("z", "x", "c", "y"))
    own_p = p_blocks.reshape(RB * BS, CW)

    lists = row_send.reshape(NZ, NX * NC * GP).astype(jnp.bfloat16)
    lists = jnp.pad(lists[:, None, :], ((0, 0), (0, PAD - 1), (0, CW - NX * NC * GP)))
    message = jnp.concatenate([jnp.broadcast_to(own_p[None], (NZ, RB * BS, CW)), lists], 1)
    far_p = lax.all_to_all(message, "z", split_axis=0, concat_axis=0, tiled=True)
    near_p = lax.all_to_all(message, "y", split_axis=0, concat_axis=0, tiled=True)

    live = jnp.arange(RB, dtype=jnp.int32)[:, None] < a_live[0]
    far = live & (a_cols >= NEAR)
    entry = jnp.where(far, a_cols - NEAR, 0)
    panel = jnp.where(far, entry // GP, OFF)
    codes = jnp.stack([panel.reshape(-1), (entry % GP).reshape(-1)]).astype(jnp.bfloat16)
    codes = jnp.pad(codes, ((0, PAD - 2), (0, SA * BS + CW - SLOTS)))
    rows = jnp.concatenate([a_blocks.reshape(RB * BS, SA * BS), own_p], 1)
    group_rows = lax.all_gather(jnp.concatenate([rows, codes], 0), "x", axis=0)
    far_p = lax.all_gather(far_p, "c", axis=0).reshape(NC * NZ, ROWS, CW)

    code = group_rows[:, RB * BS : RB * BS + 2, :SLOTS].astype(jnp.int32)
    sent = far_p[:, RB * BS, : NX * NC * GP].astype(jnp.int32)
    place = jnp.stack([my_z, my_x, my_c, a_live[0], my_y]).astype(jnp.int32)

    partial = pl.pallas_call(
        terms_kernel,
        out_shape=jax.ShapeDtypeStruct((NX, NZ, NC, CW, CW), jnp.bfloat16),
        grid_spec=pltpu.PrefetchScalarGridSpec(
            num_scalar_prefetch=5,
            grid=(NX,),
            in_specs=[
                pl.BlockSpec((1, ROWS, SA * BS + CW), lambda i, *_: (i, 0, 0)),
                pl.BlockSpec((NC * NZ, ROWS, CW), lambda i, *_: (0, 0, 0)),
                pl.BlockSpec((NY, ROWS, CW), lambda i, *_: (0, 0, 0)),
            ],
            out_specs=pl.BlockSpec((1, NZ, NC, CW, CW), lambda i, *_: (i, 0, 0, 0, 0)),
            scratch_shapes=[
                pltpu.VMEM((RB * SA // 2, CW, CW), jnp.bfloat16),
                pltpu.VMEM((NC * NZ + 1, CW, CW), jnp.float32),
                pltpu.SMEM((SLOTS + UNROLL,), jnp.int32),
            ],
        ),
        compiler_params=pltpu.CompilerParams(vmem_limit_bytes=40 * 1024 * 1024),
        cost_estimate=pl.CostEstimate(flops=2 * 10**9, bytes_accessed=12 * 10**6, transcendentals=0),
        name="terms",
    )(place, code, sent, a_cols.reshape(-1), group_need.reshape(-1), group_rows, far_p, near_p)

    parts = lax.all_to_all(
        partial.reshape(NX * NY, NC, CW, CW), ("x", "y"), split_axis=0, concat_axis=0, tiled=True
    ).reshape(NX, NY, NC, CW, CW)
    total = jnp.sum(parts.astype(jnp.float32), axis=1).astype(jnp.bfloat16)
    return total.reshape(1, NX * NC, CW, CW)


def solution(mesh):
    split = Mesh(mesh.devices.reshape(NZ, NX, NC, NY), ("z", "x", "c", "y"))
    every = ("z", "x", "c", "y")
    placed = (
        P(every, None, None),
        P(every, None, None),
        P(every, None),
        P(every),
        P(every, None, None),
        P(every, None, None),
    )
    return jax.shard_map(
        shards, mesh=split, in_specs=placed, out_specs=P(("z", "x", "c"), "y", None, None), check_vma=False
    )
```

time: 274 us -> 216 us (0.79)
  waiting for transfers between devices: 172 us -> 69.8 us
  blocking collectives: 0 us -> 95.7 us
  other arithmetic: 44.8 us -> 4.85 us
  Pallas kernels: 0 us -> 14 us
  local copies, waits for them, and re-layouts: 17.4 us -> 6.43 us
  starting transfers between devices: 15.2 us -> 6.88 us
  matrix products: 6.9 us -> 0 us
    all_to_all x0 -> x2, blocking collectives: none -> 95.7 us  [the longest x1 57 us: shards(): lax.all_to_all(partial.reshape(NX * NY, NC, CW, CW), ('x', 'y'), split_ax...]
    all_to_all x1, waiting for transfers between devices: 95.5 us -> 0.01 us  [shards(): lax.all_to_all(message, 'y', split_axis=0, concat_axis=0, tiled=True)]
    reduce_scatter x1 -> x0, waiting for transfers between devices: 39.7 us -> none  [shards(): lax.psum_scatter(running.astype(jnp.bfloat16), 'grp', scatter_dimension=0...]
    all_gather x1 -> x2, waiting for transfers between devices: 36 us -> 69.8 us  [the longest x1 60.4 us: shards(): group_rows = lax.all_gather(jnp.concatenate([rows, codes], 0), 'x', axis=0)]
    scatter-add x1 -> x0, other arithmetic: 26.5 us -> none  [accumulate(): running.at[panels.reshape(-1)]]
    pallas_call x0 -> x1, Pallas kernels: none -> 14 us  [shards(): pl.pallas_call(terms_kernel, out_shape=jax.ShapeDtypeStruct((NX, NZ, NC,...]
    gather x3 -> x0, local copies, waits for them, and re-layouts: 11 us -> none  [the longest x1 4.94 us: shards(): p_blocks[row_send[0].reshape(-1)]]
    all_to_all x1, starting transfers between devices: 15.1 us -> 6.83 us  [shards(): lax.all_to_all(message, 'y', split_axis=0, concat_axis=0, tiled=True)]
  transfers between devices with their start and end apart: 3 -> 3, of which waited for: 3 -> 2; matrix products, arithmetic and copies ran while one was open for 2% -> 1% of each run, Pallas kernels for 0% -> 0%
where the time goes in v1:
time: 216 us; the launch traced here: 212 us
  blocking collectives  95.7 us (44%)
  waiting for transfers between devices  69.8 us (32%)
  between operations  14.1 us (7%)
  Pallas kernels  14 us (6%)
  starting transfers between devices  6.88 us (3%)
  local copies, waits for them, and re-layouts  6.43 us (3%)
  other arithmetic  4.85 us (2%)
    all_gather x1, waiting for transfers between devices, shards(): group_rows = lax.all_gather(jnp.concatenate([rows, codes], 0), 'x', axis=0)  60.4 us
    all_to_all x1, blocking collectives, shards(): lax.all_to_all(partial.reshape(NX * NY, NC, CW, CW), ('x', 'y'), split_ax...  57 us
    all_to_all x1, blocking collectives, shards(): lax.all_to_all(message, 'z', split_axis=0, concat_axis=0, tiled=True)  38.8 us
    pallas_call x1, Pallas kernels, shards(): pl.pallas_call(terms_kernel, out_shape=jax.ShapeDtypeStruct((NX, NZ, NC,...  14 us
    all_gather x1, waiting for transfers between devices, shards(): far_p = lax.all_gather(far_p, 'c', axis=0).reshape(NC * NZ, ROWS, CW)  9.4 us
    all_to_all x1, starting transfers between devices, shards(): lax.all_to_all(message, 'y', split_axis=0, concat_axis=0, tiled=True)  6.83 us
  transfers between devices with their start and end apart: 3, of which 2 were waited for; matrix products, arithmetic and copies ran while one was open for 1% of the time, Pallas kernels for 0%

profile of v1, /device:TPU:1, one launch (start us, length us, event | category | flops | bytes accessed | tf_op | source)
XLA Modules:
  0.0 211.8 jit_solution(2743746858742688714)
XLA Ops:
  6.5 0.0 all-gather.7.cloned.1.call-start
  6.5 0.7 convert_element_type.29
  7.2 0.1 copy.10
  7.3 0.1 convert_element_type.34
  7.4 1.0 broadcast_in_dim.16
  8.5 1.1 fusion.1
  9.6 0.0 copy-start.4
  9.6 0.0 copy-start.2
  9.6 0.0 copy-start.3
  9.6 38.8 %all_to_all.15 = bf16[8,528,128]{2,1,0:T(8,128)(2,1)} all-to-all(bf16[8,528,128]{2,1,0:T(8,128)(2,1)} %fusion.1), channel_id=1, replica_groups=mesh['z'=8,'x'=4,'c'=2,'y'=8] {'z'}, dimensions={0} | all-to-all | bytes 2162688 | tf_op jit(solution)/shard_map/all_to_all | solution.py:93
  48.4 0.0 all-gather.7.cloned.1.call-update
  48.4 0.0 all-gather.5.cloned.1.call-start
  49.1 0.0 copy-done.4
  49.2 0.1 fusion.9
  49.2 0.1 stack_reshape.8
  49.3 0.1 stack_reshape.9
  49.4 0.0 copy-done.2
  49.4 0.0 copy-done.3
  49.5 1.1 pad_maximum_fusion
  50.6 0.0 copy-start.5
  50.6 0.0 all-gather.5.cloned.1.call-update
  50.6 6.8 %all-to-all-start.1 = ((bf16[8,528,128]{2,1,0:T(8,128)(2,1)}), bf16[8,528,128]{2,1,0:T(8,128)(2,1)S(1)}, u32[]{:S(2)}, u32[]{:S(2)}) async-start(bf16[8,528,128]{2,1,0:T(8,128)(2,1)} %fusion.1), calls=%async_computation.1 | async-start | bytes 2162688 | tf_op jit(solution)/shard_map/all_to_all | solution.py:94
  57.5 0.1 reshape.47.cols
  57.5 0.0 copy-done.5
  57.5 0.1 reshape.48.need
  57.6 0.1 stack.23.place
  57.7 9.4 %all-gather.7.cloned.1.call-done.p_ref = bf16[16,528,128]{2,1,0:T(8,128)(2,1)} async-done(((bf16[8,528,128]{2,1,0:T(8,128)(2,1)}), bf16[16,528,128]{2,1,0:T(8,128)(2,1)}) %all-gather.7.cloned.1.call-update) | async-done | bytes 2162704 | tf_op jit(solution)/shard_map/all_gather | solution.py:104
  67.1 0.8 slice.9
  67.9 60.4 %all-gather.5.cloned.1.call-done = bf16[2112,1152]{1,0:T(8,128)(2,1)} async-done(((bf16[528,1152]{1,0:T(8,128)(2,1)}), bf16[2112,1152]{1,0:T(8,128)(2,1)}) %all-gather.5.cloned.1.call-update) | async-done | bytes 4866064 | tf_op jit(solution)/shard_map/all_gather | solution.py:103
  128.3 0.7 slice_convert_fusion.code
  129.0 0.0 all-to-all-done.1.near_ref
  129.0 0.0 copy-start
  129.0 2.4 %copy-done = bf16[2112,1152]{1,0:T(8,128)(2,1)S(1)} copy-done((bf16[2112,1152]{1,0:T(8,128)(2,1)S(1)}, bf16[2112,1152]{1,0:T(8,128)(2,1)}, u32[]{:S(2)}) %copy-start) | copy-done | bytes 4866072
  131.4 0.0 copy-start.1
  131.4 1.6 copy-done.1
  133.0 14.0 %terms.1 = bf16[4,8,2,128,128]{4,3,2,1,0:T(8,128)(2,1)S(1)} custom-call(s32[5]{0:T(128)S(1)} %stack.23.place, s32[4,2,128]{2,1,0:T(2,128)S(1)} %slice_convert_fusion.code, s32[16,48]{1,0:T(8,128)S(1)} %fusion.11.sent, s32[128]{0:T(128)S(1)} %reshape.47.cols, s32[64]{0:T(128)S(1)} %reshape.48.need, bf16[4,528,1152]{2,1,0:T(8,128)(2,1)S(1)} %bitcast.20, ...), custom_call_target="tpu_custom_call" | custom-call | flops 2000000000 | bytes 12000000 | tf_op jit(solution)/shard_map/terms/pallas_call | solution.py:110
  147.0 57.0 %all_to_all.16 = bf16[32,2,128,128]{3,2,1,0:T(8,128)(2,1)S(1)} all-to-all(bf16[32,2,128,128]{3,2,1,0:T(8,128)(2,1)S(1)} %bitcast.18), channel_id=1, replica_groups=mesh['z'=8,'x'=4,'c'=2,'y'=8] {'x','y'}, dimensions={0} | all-to-all | bytes 4194304 | tf_op jit(solution)/shard_map/all_to_all | solution.py:133
  204.0 1.1 bitcast_reduce_fusion
  (3 shorter events, 0.0 us)
Async XLA Ops:
  6.5 60.6 %all-gather.7.cloned.1.call-start = ((), (), s32[]{:S(2)}) async-start(), calls=%async_computation.4 | async-start | bytes 3244032 | tf_op jit(solution)/shard_map/all_gather | solution.py:104
  9.6 39.5 %copy-start.4 = (s32[8,16]{1,0:T(8,128)S(1)}, s32[8,16]{1,0:T(8,128)}, u32[]{:S(2)}) copy-start(s32[8,16]{1,0:T(8,128)} %param.8) | copy-start | bytes 1540
  9.6 39.8 %copy-start.2 = (bf16[8,64,1024]{2,1,0:T(8,128)(2,1)S(1)}, bf16[8,64,1024]{2,1,0:T(8,128)(2,1)}, u32[]{:S(2)}) copy-start(bf16[8,64,1024]{2,1,0:T(8,128)(2,1)} %param.6) | copy-start | bytes 3145732
  9.6 39.8 %copy-start.3 = (bf16[8,64,128]{2,1,0:T(8,128)(2,1)S(1)}, bf16[8,64,128]{2,1,0:T(8,128)(2,1)}, u32[]{:S(2)}) copy-start(bf16[8,64,128]{2,1,0:T(8,128)(2,1)} %param.7) | copy-start | bytes 393220
  48.4 79.8 %all-gather.5.cloned.1.call-start = ((), (), s32[]{:S(2)}) async-start(), calls=%async_computation.3 | async-start | bytes 6082560 | tf_op jit(solution)/shard_map/all_gather | solution.py:103
  50.6 6.9 %copy-start.5 = (s32[1,8,8]{2,1,0:T(8,128)S(1)}, s32[1,8,8]{2,1,0:T(8,128)}, u32[]{:S(2)}) copy-start(s32[1,8,8]{2,1,0:T(8,128)} %param.10) | copy-start | bytes 772
  50.6 78.3 %all-to-all-start.1 = ((bf16[8,528,128]{2,1,0:T(8,128)(2,1)}), bf16[8,528,128]{2,1,0:T(8,128)(2,1)S(1)}, u32[]{:S(2)}, u32[]{:S(2)}) async-start(bf16[8,528,128]{2,1,0:T(8,128)(2,1)} %fusion.1), calls=%async_computation.1 | async-start | bytes 2162688 | tf_op jit(solution)/shard_map/all_to_all | solution.py:94
  129.0 2.4 %copy-start = (bf16[2112,1152]{1,0:T(8,128)(2,1)S(1)}, bf16[2112,1152]{1,0:T(8,128)(2,1)}, u32[]{:S(2)}) copy-start(bf16[2112,1152]{1,0:T(8,128)(2,1)} %all-gather.5.cloned.1.call-done) | copy-start | bytes 14598148
  131.4 1.6 copy-start.1
Sparse Core Ops, SparseCore 0:
  48.6 18.5 all-gather.6
  69.2 59.0 all-gather.4

commit v2 on v0

v2 whole, which is shorter than its diff:
```python
import jax
import jax.numpy as jnp
from jax import lax
from jax.experimental import pallas as pl
from jax.experimental.pallas import tpu as pltpu
from jax.sharding import Mesh, PartitionSpec as P

NZ, NX, NC, NY = 8, 4, 2, 8
RB, BS, CW, SA = 8, 64, 128, 16
GP = 6
NEAR = RB + NY * RB
SLOTS = RB * SA
PAD = 16
PROWS = RB * BS
ROWS = PROWS + PAD
AW = SA * BS + CW
UNROLL = 4
OFF = 255
FLAG = 20
BF16, F32, I32 = jnp.bfloat16, jnp.float32, jnp.int32


def pack_kernel(live, a_ref, p_ref, cols, lists, own_ref, message_ref):
    own_ref[:PROWS, : SA * BS] = a_ref[...]
    own_ref[:PROWS, SA * BS :] = p_ref[...]
    message_ref[:PROWS, :] = p_ref[...]
    listed = jnp.concatenate([lists[z] for z in range(NZ)], 1)
    listed = jnp.concatenate([listed, jnp.zeros((NX * NC, CW - NZ * GP), I32)], 1)
    message_ref[PROWS:, :] = jnp.concatenate([listed, jnp.zeros_like(listed)], 0).astype(F32).astype(BF16)
    entry = cols[...] - NEAR
    far = (entry >= 0) & (lax.broadcasted_iota(I32, (RB, SA), 0) < live[0])
    entry = jnp.where(far, entry, 0)
    panel = (entry * 10923) >> 16
    codes = jnp.concatenate([jnp.where(far, panel, OFF), entry - panel * GP], 0)
    own_ref[PROWS:, :] = jnp.zeros((PAD, AW), BF16)
    own_ref[PROWS:, :SA] = codes.astype(F32).astype(BF16)


def terms_kernel(place, need, cols, *refs):
    groups_hbm, refs = refs[:NX], refs[NX:]
    here_hbm, one_hbm, two_hbm, three_hbm, four_hbm, crossed_hbm, near_hbm = refs[:7]
    o_ref, a_ref, p_ref, near_ref, left, acc, items_v, sent_v, items, sent, todo, sems = refs[7:]
    my_z, my_x, my_c, my_y, live, odd_z = (place[i] for i in range(6))
    back = 2 * my_c - 1
    copies = [pltpu.make_async_copy(groups_hbm[turn], a_ref.at[turn], sems.at[turn]) for turn in range(NX)]
    sources = [(here_hbm, 0), (one_hbm, back), (two_hbm, 2 * back), (three_hbm, 3 * back), (four_hbm, 4)]
    sources += [(crossed_hbm.at[s], -(s + 1) * back) for s in range(3)]
    tables = [
        pltpu.make_async_copy(source, p_ref.at[(my_z + step) & (NZ - 1)], sems.at[NX + at])
        for at, (source, step) in enumerate(sources)
    ]
    near_copy = pltpu.make_async_copy(near_hbm, near_ref, sems.at[NX + NZ])
    for copy in copies[:1] + tables + [near_copy] + copies[1:]:
        copy.start()
    slots = lax.broadcasted_iota(I32, (RB, CW), 0) * SA + lax.broadcasted_iota(I32, (RB, CW), 1)
    moves = [
        pltpu.make_async_copy(items_v.at[turn], items.at[turn], sems.at[NX + NZ + 1 + turn]) for turn in range(NX + 1)
    ]
    list_move = pltpu.make_async_copy(sent_v, sent, sems.at[2 * NX + NZ + 2])

    entry = cols[...]
    close = (entry < NEAR) & (lax.broadcasted_iota(I32, (RB, SA), 0) < live) & ((my_z & 1) == odd_z)
    items_v[NX, :, :SA] = jnp.where(close, slots[:, :SA] | (entry << 7) | (1 << FLAG), 0)
    moves[NX].start()
    acc[...] = jnp.zeros_like(acc)

    for turn in range(NX):
        copies[turn].wait()
        code = a_ref[turn, pl.ds(PROWS, PAD), :CW].astype(F32).astype(I32)
        panel, listed = code[:RB], code[RB:]
        mine = (panel < OFF) & (((panel >> 1) & (NX - 1)) == my_x) & (((panel >> 3) & 1) == odd_z)
        source = (panel >> 3) * NC + (panel & 1)
        item = (slots + turn * SLOTS) | (listed << 9) | (source << 12) | (1 << FLAG)
        items_v[turn] = jnp.where(mine, item, 0)
        moves[turn].start()
        for n in range(RB):
            rows = pl.ds(n * BS, BS)
            product = lax.dot_general(
                a_ref[turn, rows, SA * BS :], a_ref[turn, rows, : SA * BS], (((0,), (0,)), ((), ())),
                preferred_element_type=F32,
            ).astype(BF16)
            for pair in range(SA // 2):
                left[(turn * RB + n) * (SA // 2) + pair] = product[:, pair * CW : (pair + 1) * CW]
    for copy in tables:
        copy.wait()
    both = p_ref[:, :, pl.ds(PROWS, PAD), :].astype(F32)[:, :, : NX * NC].astype(I32)
    sent_v[...] = jnp.where(my_c == 0, both[:, :, :NX], both[:, :, NX:]).reshape(NZ, NC * NX, CW)
    list_move.start()

    def add_terms(first, turns, block_of, panel_of):
        def pick(at, count):
            for s in range(SA):
                item = items[first + (at >> 3), at & 7, s]
                todo[count] = item
                count = count + (item >> FLAG)
            return count

        count = lax.fori_loop(0, turns * RB, pick, 0)
        for u in range(UNROLL):
            todo[count + u] = 0

        def body(step, unused):
            found = []
            for u in range(UNROLL):
                item = todo[step * UNROLL + u]
                slot = item & (SLOTS * turns - 1)
                block = block_of(item)
                odd = (slot & 1) == 1
                zero = jnp.zeros_like(block)
                right = jnp.concatenate([jnp.where(odd, zero, block), jnp.where(odd, block, zero)], 0)
                term = jnp.dot(left[slot >> 1], right, preferred_element_type=F32)
                found.append((jnp.where((item >> FLAG) == 1, panel_of(item), NX * NZ), term))
            for panel, term in found:
                acc[panel] += term
            return 0

        lax.fori_loop(0, (count + UNROLL - 1) // UNROLL, body, 0)

    def near_block(item):
        entry = (item >> 7) & 127
        listed = jnp.maximum(entry - RB, 0)
        member = jnp.where(entry < RB, my_y, listed >> 3)
        row = jnp.where(entry < RB, entry, need[listed])
        return near_ref[member, pl.ds(pl.multiple_of(row * BS, BS), BS), :]

    def far_block(item):
        panel = (item >> 12) & 15
        group = (my_x - ((item >> 7) & 3)) & (NX - 1)
        row = sent[panel >> 1, (panel & 1) * NX + group, my_z * GP + ((item >> 9) & 7)]
        return p_ref[panel >> 1, panel & 1, pl.ds(pl.multiple_of(row * BS, BS), BS), :]

    near_copy.wait()
    moves[NX].wait()
    add_terms(NX, 1, near_block, lambda item: (my_z >> 1) * NC + my_c)
    for turn in range(NX):
        moves[turn].wait()
    list_move.wait()
    add_terms(0, NX, far_block, lambda item: ((item >> 7) & 3) * NZ + ((item >> 14) & 3) * NC + ((item >> 12) & 1))
    for turn in range(NX):
        group = (my_x - turn) & (NX - 1)
        for at in range(NZ):
            o_ref[group, at // NC, at % NC] = acc[turn * NZ + at].astype(BF16)


def hop(array, axis, size, step):
    return lax.ppermute(array, axis, [(i, (i + step) % size) for i in range(size)])


def shards(a_blocks, p_blocks, a_cols, a_live, group_need, row_send):
    my_z, my_x, my_c, my_y = (lax.axis_index(axis).astype(I32) for axis in ("z", "x", "c", ("yh", "yl")))
    own_p = p_blocks.reshape(PROWS, CW)
    hbm, vmem, smem = (pl.BlockSpec(memory_space=space) for space in (pl.ANY, pltpu.VMEM, pltpu.SMEM))

    by_core = row_send.reshape(NZ, NX, NC, GP).transpose(0, 2, 1, 3).reshape(NZ, NC * NX, GP)
    own, message = pl.pallas_call(
        pack_kernel,
        out_shape=(jax.ShapeDtypeStruct((ROWS, AW), BF16), jax.ShapeDtypeStruct((ROWS, CW), BF16)),
        in_specs=[smem, vmem, vmem, vmem, vmem],
        out_specs=(vmem, vmem),
        name="pack",
    )(a_live, a_blocks.reshape(PROWS, SA * BS), own_p, a_cols, by_core)

    low = hop(own, "x", NX, 1)
    high = hop(own, "x", NX, -1)
    near_p = lax.all_to_all(
        jnp.broadcast_to(own_p[None], (NY, PROWS, CW)), ("yh", "yl"), split_axis=0, concat_axis=0, tiled=True
    )

    around = [(z * NC + c, (z + 1 - 2 * c) % NZ * NC + c) for z in range(NZ) for c in range(NC)]
    beside = hop(message, "c", NC, 1)
    here = jnp.where(my_c == 0, jnp.stack([message, beside]), jnp.stack([beside, message]))
    one = lax.ppermute(here, ("z", "c"), around)
    two = lax.ppermute(one, ("z", "c"), around)
    three = lax.ppermute(two, ("z", "c"), around)
    four = lax.ppermute(three, ("z", "c"), around)
    crossed = hop(jnp.stack([one, two, three]), "c", NC, 1)
    last = lax.ppermute(
        jnp.where(my_c == 0, low, high),
        ("x", "c"),
        [(x * NC + c, (x + 1 - 2 * c) % NX * NC + c) for x in range(NX) for c in range(NC)],
    )

    def terms(odd_z):
        return pl.pallas_call(
            terms_kernel,
            out_shape=jax.ShapeDtypeStruct((NX, NZ // 2, NC, CW, CW), BF16),
            in_specs=[smem, smem, vmem] + [hbm] * 11,
            out_specs=vmem,
            scratch_shapes=[
                pltpu.VMEM((NX, ROWS, AW), BF16),
                pltpu.VMEM((NZ, NC, ROWS, CW), BF16),
                pltpu.VMEM((NY, PROWS, CW), BF16),
                pltpu.VMEM((NX * SLOTS // 2, CW, CW), BF16),
                pltpu.VMEM((NX * NZ + 1, CW, CW), F32),
                pltpu.VMEM((NX + 1, RB, CW), I32),
                pltpu.VMEM((NZ, NC * NX, CW), I32),
                pltpu.SMEM((NX + 1, RB, CW), I32),
                pltpu.SMEM((NZ, NC * NX, CW), I32),
                pltpu.SMEM((NX * SLOTS + UNROLL,), I32),
                pltpu.SemaphoreType.DMA((2 * NX + NZ + 3,)),
            ],
            compiler_params=pltpu.CompilerParams(vmem_limit_bytes=56 * 1024 * 1024),
            cost_estimate=pl.CostEstimate(flops=2 * 10**9, bytes_accessed=12 * 10**6, transcendentals=0),
            name="terms",
        )(
            jnp.stack([my_z, my_x, my_c, my_y, a_live[0], odd_z]), group_need.reshape(-1), a_cols,
            own, low, last, high, here, one, two, three, four, crossed, near_p,
        )

    pairs = [
        (c * NY + y, c * NY + (y + 1 - 2 * ((y + c) & 1)) % NY) for c in range(NC) for y in range(NY)
    ]
    given = lax.ppermute(terms(1 - (my_y & 1)), ("c", "yh", "yl"), pairs)
    kept = terms(my_y & 1)
    partial = (kept.astype(F32) + given.astype(F32)).astype(BF16)

    parts = lax.all_to_all(
        partial.reshape(NX * NY // 2, NC, CW, CW), ("x", "yh"), split_axis=0, concat_axis=0, tiled=True
    ).reshape(NX, NY // 2, NC, CW, CW)
    total = jnp.sum(parts.astype(F32), axis=1).astype(BF16)
    return total.reshape(1, NX * NC, CW, CW)


def solution(mesh):
    split = Mesh(mesh.devices.reshape(NZ, NX, NC, NY // 2, 2), ("z", "x", "c", "yh", "yl"))
    every = ("z", "x", "c", "yh", "yl")
    placed = (
        P(every, None, None),
        P(every, None, None),
        P(every, None),
        P(every),
        P(every, None, None),
        P(every, None, None),
    )
    return jax.shard_map(
        shards, mesh=split, in_specs=placed, out_specs=P(("z", "x", "c"), ("yh", "yl"), None, None), check_vma=False
    )
```

time: 274 us -> 141 us (0.51); the launches traced: 270 us -> 140 us
  waiting for transfers between devices: 172 us -> 8.17 us
  starting transfers between devices: 15.2 us -> 58.3 us
  other arithmetic: 44.8 us -> 6.66 us
  blocking collectives: 0 us -> 36.3 us
  Pallas kernels: 0 us -> 24.1 us
  between operations: 14.2 us -> 0.92 us
  local copies, waits for them, and re-layouts: 17.4 us -> 6.07 us
  matrix products: 6.9 us -> 0 us
    all_to_all x1, waiting for transfers between devices: 95.5 us -> 0.01 us  [shards(): lax.all_to_all(jnp.broadcast_to(own_p[None], (NY, PROWS, CW)), ('yh', 'yl...]
    ppermute x0 -> x10, starting transfers between devices: none -> 51.5 us  [the longest x4 19.7 us: hop(): lax.ppermute(array, axis, [(i, (i + step) % size) for i in range(size)])]
    reduce_scatter x1 -> x0, waiting for transfers between devices: 39.7 us -> none  [shards(): lax.psum_scatter(running.astype(jnp.bfloat16), 'grp', scatter_dimension=0...]
    all_to_all x0 -> x1, blocking collectives: none -> 36.3 us  [shards(): lax.all_to_all(partial.reshape(NX * NY // 2, NC, CW, CW), ('x', 'yh'), sp...]
    all_gather x1 -> x0, waiting for transfers between devices: 36 us -> none  [shards(): panel_rows = lax.all_gather(p_blocks, 'grp', axis=0, tiled=True)]
    scatter-add x1 -> x0, other arithmetic: 26.5 us -> none  [accumulate(): running.at[panels.reshape(-1)]]
    pallas_call x0 -> x3, Pallas kernels: none -> 24.1 us  [the longest x2 21.6 us: terms(): pl.pallas_call(terms_kernel, out_shape=jax.ShapeDtypeStruct((NX, NZ // 2,...]
    gather x3 -> x0, local copies, waits for them, and re-layouts: 11 us -> none  [the longest x1 4.94 us: shards(): p_blocks[row_send[0].reshape(-1)]]
  transfers between devices with their start and end apart: 3 -> 11, of which waited for: 3 -> 4; matrix products, arithmetic and copies ran while one was open for 2% -> 5% of each run, Pallas kernels for 0% -> 8%
where the time goes in v2:
time: 141 us; the launch traced here: 140 us
  starting transfers between devices  58.3 us (41%)
  blocking collectives  36.3 us (26%)
  Pallas kernels  24.1 us (17%)
  waiting for transfers between devices  8.17 us (6%)
  other arithmetic  6.66 us (5%)
  local copies, waits for them, and re-layouts  6.07 us (4%)
    all_to_all x1, blocking collectives, shards(): lax.all_to_all(partial.reshape(NX * NY // 2, NC, CW, CW), ('x', 'yh'), sp...  36.3 us
    pallas_call x2, Pallas kernels, terms(): pl.pallas_call(terms_kernel, out_shape=jax.ShapeDtypeStruct((NX, NZ // 2,...  21.6 us
    ppermute x4, starting transfers between devices, hop(): lax.ppermute(array, axis, [(i, (i + step) % size) for i in range(size)])  19.7 us
    ppermute x1, starting transfers between devices, shards(): three = lax.ppermute(two, ('z', 'c'), around)  9.45 us
    all_to_all x1, starting transfers between devices, shards(): lax.all_to_all(jnp.broadcast_to(own_p[None], (NY, PROWS, CW)), ('yh', 'yl...  6.82 us
    ppermute x1, starting transfers between devices, shards(): one = lax.ppermute(here, ('z', 'c'), around)  6.03 us
    ppermute x1, starting transfers between devices, shards(): given = lax.ppermute(terms(1 - (my_y & 1)), ('c', 'yh', 'yl'), pairs)  5.5 us
    ppermute x1, starting transfers between devices, shards(): lax.ppermute(jnp.where(my_c == 0, low, high), ('x', 'c'), [(x * NC + c, (...  4.97 us
  transfers between devices with their start and end apart: 11, of which 4 were waited for; matrix products, arithmetic and copies ran while one was open for 5% of the time, Pallas kernels for 8%

profile of v2, /device:TPU:1, one launch (start us, length us, event | category | flops | bytes accessed | tf_op | source)
XLA Modules:
  0.0 140.5 jit_solution(10251815617500501905)
XLA Ops:
  0.0 0.0 copy-start.7
  0.7 0.8 copy.8
  1.5 0.6 copy.9
  2.1 2.5 %pack.1 = (bf16[528,1152]{1,0:T(8,128)(2,1)}, bf16[528,128]{1,0:T(8,128)(2,1)}) custom-call(s32[1]{0:T(128)S(6)} %copy.10.live, bf16[512,1024]{1,0:T(8,128)(2,1)} %bitcast.24, bf16[512,128]{1,0:T(8,128)(2,1)} %bitcast.25, s32[8,16]{1,0:T(8,128)} %cols.5, s32[8,8,6]{2,1,0:T(8,128)} %bitcast.29), custom_call_target="tpu_custom_call" | custom-call | tf_op jit(solution)/shard_map/pack/pallas_call | solution.py:155
  4.5 5.2 %collective-permute-start.1 = (bf16[528,1152]{1,0:T(8,128)(2,1)}, bf16[528,1152]{1,0:T(8,128)(2,1)S(1)}, u32[]{:S(2)}, u32[]{:S(2)}) collective-permute-start(bf16[528,1152]{1,0:T(8,128)(2,1)} %get-tuple-element.7.refs_0_), channel_id=1, source_target_pairs={{0,48},{16,0},{32,16},{48,32},{1,49},{17,1},{33,17},{49,33},{2,50}... | collective-permute-start | bytes 3649544 | tf_op jit(solution)/shard_map/ppermute | solution.py:146
  9.8 1.9 %collective-permute-start = (bf16[528,1152]{1,0:T(8,128)(2,1)}, bf16[528,1152]{1,0:T(8,128)(2,1)S(1)}, u32[]{:S(2)}, u32[]{:S(2)}) collective-permute-start(bf16[528,1152]{1,0:T(8,128)(2,1)} %get-tuple-element.7.refs_0_), channel_id=1, source_target_pairs={{0,16},{16,32},{32,48},{48,0},{1,17},{17,33},{33,49},{49,1},{2,18}... | collective-permute-start | bytes 3649544 | tf_op jit(solution)/shard_map/ppermute | solution.py:146
  11.7 7.5 %collective-permute-start.3 = (bf16[528,128]{1,0:T(8,128)(2,1)}, bf16[528,128]{1,0:T(8,128)(2,1)S(1)}, u32[]{:S(2)}, u32[]{:S(2)}) collective-permute-start(bf16[528,128]{1,0:T(8,128)(2,1)} %get-tuple-element.8), channel_id=1, source_target_pairs={{0,8},{8,0},{1,9},{9,1},{2,10},{10,2},{3,11},{11,3},{4,12},{12,4},... | collective-permute-start | bytes 405512 | tf_op jit(solution)/shard_map/ppermute | solution.py:146
  19.2 1.2 collective-permute-done.3
  20.4 1.7 %maximum_select_fusion.refs_4_ = bf16[2,528,128]{2,1,0:T(8,128)(2,1)} fusion(bf16[1,528,128]{2,1,0:T(8,128)(2,1)S(1)} %bitcast.28, bf16[1,528,128]{2,1,0:T(8,128)(2,1)} %bitcast.27, pred[]{:T(512)S(6)} %eq.4), kind=kLoop, calls=%fused_computation.4 | loop fusion | flops 405504 | bytes 540673 | tf_op jit(solution)/shard_map/jit(_where)/select_n | solution.py:171
  22.1 6.0 %collective-permute-start.4 = (bf16[2,528,128]{2,1,0:T(8,128)(2,1)}, bf16[2,528,128]{2,1,0:T(8,128)(2,1)}, u32[]{:S(2)}, u32[]{:S(2)}) collective-permute-start(bf16[2,528,128]{2,1,0:T(8,128)(2,1)} %maximum_select_fusion.refs_4_), channel_id=1, source_target_pairs={{0,64},{8,456},{64,128},{72,8},{128,192},{136,72},{192,256},{200,1... | collective-permute-start | bytes 811016 | tf_op jit(solution)/shard_map/ppermute | solution.py:172
  28.1 0.0 copy-done.7
  28.2 1.1 broadcast_in_dim.2
  29.3 6.8 %all-to-all-start = ((bf16[8,512,128]{2,1,0:T(8,128)(2,1)}), bf16[8,512,128]{2,1,0:T(8,128)(2,1)S(1)}, u32[]{:S(2)}, u32[]{:S(2)}) async-start(bf16[8,512,128]{2,1,0:T(8,128)(2,1)} %broadcast_in_dim.2), calls=%async_computation | async-start | bytes 2097152 | tf_op jit(solution)/shard_map/all_to_all | solution.py:165
  36.1 0.0 collective-permute-done.4.refs_5_
  36.1 2.2 %collective-permute-start.5 = (bf16[2,528,128]{2,1,0:T(8,128)(2,1)}, bf16[2,528,128]{2,1,0:T(8,128)(2,1)S(1)}, u32[]{:S(2)}, u32[]{:S(2)}) collective-permute-start(bf16[2,528,128]{2,1,0:T(8,128)(2,1)} %collective-permute-done.4.refs_5_), channel_id=1, source_target_pairs={{0,64},{8,456},{64,128},{72,8},{128,192},{136,72},{192,256},{200,1... | collective-permute-start | bytes 811016 | tf_op jit(solution)/shard_map/ppermute | solution.py:173
  38.3 0.0 collective-permute-done.1.refs_3_
  38.3 0.0 copy-start
  38.3 0.0 collective-permute-done.refs_1_
  38.4 0.0 copy-start.1
  38.4 1.3 broadcast_select_fusion
  39.7 0.1 copy-done
  39.8 0.3 copy-done.1
  40.1 0.0 copy-start.8
  40.1 5.0 %collective-permute-start.2 = (bf16[528,1152]{1,0:T(8,128)(2,1)}, bf16[528,1152]{1,0:T(8,128)(2,1)}, u32[]{:S(2)}, u32[]{:S(2)}) collective-permute-start(bf16[528,1152]{1,0:T(8,128)(2,1)} %broadcast_select_fusion), channel_id=1, source_target_pairs={{0,16},{8,56},{16,32},{24,8},{32,48},{40,24},{48,0},{56,40},{1,17}... | collective-permute-start | bytes 3649544 | tf_op jit(solution)/shard_map/ppermute | solution.py:177
  45.1 0.0 collective-permute-done.5.refs_6_
  45.1 0.0 copy-start.4
  45.1 9.5 %collective-permute-start.6 = (bf16[2,528,128]{2,1,0:T(8,128)(2,1)S(1)}, bf16[2,528,128]{2,1,0:T(8,128)(2,1)S(1)}, u32[]{:S(2)}, u32[]{:S(2)}) collective-permute-start(bf16[2,528,128]{2,1,0:T(8,128)(2,1)S(1)} %collective-permute-done.5.refs_6_), channel_id=1, source_target_pairs={{0,64},{8,456},{64,128},{72,8},{128,192},{136,72},{192,256},{200,1... | collective-permute-start | bytes 811016 | tf_op jit(solution)/shard_map/ppermute | solution.py:174
  54.6 3.4 %collective-permute-done.6.refs_7_ = bf16[2,528,128]{2,1,0:T(8,128)(2,1)S(1)} collective-permute-done((bf16[2,528,128]{2,1,0:T(8,128)(2,1)S(1)}, bf16[2,528,128]{2,1,0:T(8,128)(2,1)S(1)}, u32[]{:S(2)}, u32[]{:S(2)}) %collective-permute-start.6) | collective-permute-done | bytes 270368 | tf_op jit(solution)/shard_map/ppermute | solution.py:174
  58.0 0.0 copy-start.5
  58.0 0.0 copy-done.4
  58.0 1.1 pad_maximum_fusion
  59.1 5.1 %collective-permute-start.8 = (bf16[3,2,528,128]{3,2,1,0:T(8,128)(2,1)S(1)}, bf16[3,2,528,128]{3,2,1,0:T(8,128)(2,1)S(1)}, u32[]{:S(2)}, u32[]{:S(2)}) collective-permute-start(bf16[3,2,528,128]{3,2,1,0:T(8,128)(2,1)S(1)} %pad_maximum_fusion), channel_id=1, source_target_pairs={{0,8},{8,0},{1,9},{9,1},{2,10},{10,2},{3,11},{11,3},{4,12},{12,4},... | collective-permute-start | bytes 2433032 | tf_op jit(solution)/shard_map/ppermute | solution.py:146
  64.2 3.6 %collective-permute-start.7 = (bf16[2,528,128]{2,1,0:T(8,128)(2,1)S(1)}, bf16[2,528,128]{2,1,0:T(8,128)(2,1)S(1)}, u32[]{:S(2)}, u32[]{:S(2)}) collective-permute-start(bf16[2,528,128]{2,1,0:T(8,128)(2,1)S(1)} %collective-permute-done.6.refs_7_), channel_id=1, source_target_pairs={{0,64},{8,456},{64,128},{72,8},{128,192},{136,72},{192,256},{200,1... | collective-permute-start | bytes 811016 | tf_op jit(solution)/shard_map/ppermute | solution.py:175
  67.9 0.0 copy-done.8
  67.9 0.6 reshape.26.need
  68.5 0.6 stack.69.place
  69.1 2.6 %collective-permute-done.7.refs_8_ = bf16[2,528,128]{2,1,0:T(8,128)(2,1)S(1)} collective-permute-done((bf16[2,528,128]{2,1,0:T(8,128)(2,1)S(1)}, bf16[2,528,128]{2,1,0:T(8,128)(2,1)S(1)}, u32[]{:S(2)}, u32[]{:S(2)}) %collective-permute-start.7) | collective-permute-done | bytes 270368 | tf_op jit(solution)/shard_map/ppermute | solution.py:175
  71.7 0.0 copy-start.6
  71.7 0.0 collective-permute-done.8.refs_9_
  71.7 0.0 copy-start.3
  71.7 0.0 all-to-all-done.refs_10_
  71.7 0.0 copy-start.2
  71.7 0.0 collective-permute-done.2.refs_2_
  71.7 0.0 copy-done.5
  71.8 0.7 copy-done.6
  72.4 0.3 copy-done.3
  72.8 0.3 copy-done.2
  73.1 10.8 %terms.3 = bf16[4,4,2,128,128]{4,3,2,1,0:T(8,128)(2,1)} custom-call(s32[6]{0:T(128)} %stack.69.place, s32[64]{0:T(128)} %reshape.26.need, s32[8,16]{1,0:T(8,128)} %cols.5, bf16[528,1152]{1,0:T(8,128)(2,1)} %get-tuple-element.7.refs_0_, bf16[528,1152]{1,0:T(8,128)(2,1)} %copy-done.1, bf16[528,1152]{1,0:T(8,128)(2,1)} %collective-permute-done.2.refs_2_, ...), custom_call_target="tpu_custom_call" | custom-call | flops 2000000000 | bytes 12000000 | tf_op jit(solution)/shard_map/terms/pallas_call | solution.py:184
  83.9 5.5 %collective-permute-start.9 = (bf16[4,4,2,128,128]{4,3,2,1,0:T(8,128)(2,1)}, bf16[4,4,2,128,128]{4,3,2,1,0:T(8,128)(2,1)S(1)}, u32[]{:S(2)}, u32[]{:S(2)}) collective-permute-start(bf16[4,4,2,128,128]{4,3,2,1,0:T(8,128)(2,1)} %terms.3), channel_id=1, source_target_pairs={{0,1},{1,0},{2,3},{3,2},{4,5},{5,4},{6,7},{7,6},{8,15},{9,10},{10,... | collective-permute-start | bytes 3145736 | tf_op jit(solution)/shard_map/ppermute | solution.py:213
  89.4 0.6 stack.59.place
  90.0 10.8 %terms.2 = bf16[4,4,2,128,128]{4,3,2,1,0:T(8,128)(2,1)} custom-call(s32[6]{0:T(128)} %stack.59.place, s32[64]{0:T(128)} %reshape.26.need, s32[8,16]{1,0:T(8,128)} %cols.5, bf16[528,1152]{1,0:T(8,128)(2,1)} %get-tuple-element.7.refs_0_, bf16[528,1152]{1,0:T(8,128)(2,1)} %copy-done.1, bf16[528,1152]{1,0:T(8,128)(2,1)} %collective-permute-done.2.refs_2_, ...), custom_call_target="tpu_custom_call" | custom-call | flops 2000000000 | bytes 12000000 | tf_op jit(solution)/shard_map/terms/pallas_call | solution.py:184
  100.8 1.0 collective-permute-done.9
  101.8 1.6 %add_convert_fusion = bf16[4,4,2,128,128]{4,3,2,1,0:T(8,128)(2,1)S(1)} fusion(bf16[4,4,2,128,128]{4,3,2,1,0:T(8,128)(2,1)S(1)} %collective-permute-done.9, bf16[4,4,2,128,128]{4,3,2,1,0:T(8,128)(2,1)} %terms.2), kind=kLoop, calls=%fused_computation | loop fusion | flops 2097152 | bytes 3145728 | tf_op jit(solution)/shard_map/convert_element_type | solution.py:215
  103.4 36.3 %all_to_all.10 = bf16[16,2,128,128]{3,2,1,0:T(8,128)(2,1)S(1)} all-to-all(bf16[16,2,128,128]{3,2,1,0:T(8,128)(2,1)S(1)} %bitcast.21), channel_id=1, replica_groups=mesh['z'=8,'x'=4,'c'=2,'yh'=4,'yl'=2] {'x','yh'}, dimensions={0} | all-to-all | bytes 2097152 | tf_op jit(solution)/shard_map/all_to_all | solution.py:217
  139.6 0.9 bitcast_reduce_fusion
Async XLA Ops:
  0.0 28.1 %copy-start.7 = (bf16[8,64,128]{2,1,0:T(8,128)(2,1)S(1)}, bf16[8,64,128]{2,1,0:T(8,128)(2,1)}, u32[]{:S(2)}) copy-start(bf16[8,64,128]{2,1,0:T(8,128)(2,1)} %param.7) | copy-start | bytes 393220
  4.5 33.8 %collective-permute-start.1 = (bf16[528,1152]{1,0:T(8,128)(2,1)}, bf16[528,1152]{1,0:T(8,128)(2,1)S(1)}, u32[]{:S(2)}, u32[]{:S(2)}) collective-permute-start(bf16[528,1152]{1,0:T(8,128)(2,1)} %get-tuple-element.7.refs_0_), channel_id=1, source_target_pairs={{0,48},{16,0},{32,16},{48,32},{1,49},{17,1},{33,17},{49,33},{2,50}... | collective-permute-start | bytes 3649544 | tf_op jit(solution)/shard_map/ppermute | solution.py:146
  9.8 28.6 %collective-permute-start = (bf16[528,1152]{1,0:T(8,128)(2,1)}, bf16[528,1152]{1,0:T(8,128)(2,1)S(1)}, u32[]{:S(2)}, u32[]{:S(2)}) collective-permute-start(bf16[528,1152]{1,0:T(8,128)(2,1)} %get-tuple-element.7.refs_0_), channel_id=1, source_target_pairs={{0,16},{16,32},{32,48},{48,0},{1,17},{17,33},{33,49},{49,1},{2,18}... | collective-permute-start | bytes 3649544 | tf_op jit(solution)/shard_map/ppermute | solution.py:146
  11.7 8.7 %collective-permute-start.3 = (bf16[528,128]{1,0:T(8,128)(2,1)}, bf16[528,128]{1,0:T(8,128)(2,1)S(1)}, u32[]{:S(2)}, u32[]{:S(2)}) collective-permute-start(bf16[528,128]{1,0:T(8,128)(2,1)} %get-tuple-element.8), channel_id=1, source_target_pairs={{0,8},{8,0},{1,9},{9,1},{2,10},{10,2},{3,11},{11,3},{4,12},{12,4},... | collective-permute-start | bytes 405512 | tf_op jit(solution)/shard_map/ppermute | solution.py:146
  22.1 14.0 %collective-permute-start.4 = (bf16[2,528,128]{2,1,0:T(8,128)(2,1)}, bf16[2,528,128]{2,1,0:T(8,128)(2,1)}, u32[]{:S(2)}, u32[]{:S(2)}) collective-permute-start(bf16[2,528,128]{2,1,0:T(8,128)(2,1)} %maximum_select_fusion.refs_4_), channel_id=1, source_target_pairs={{0,64},{8,456},{64,128},{72,8},{128,192},{136,72},{192,256},{200,1... | collective-permute-start | bytes 811016 | tf_op jit(solution)/shard_map/ppermute | solution.py:172
  29.3 42.4 %all-to-all-start = ((bf16[8,512,128]{2,1,0:T(8,128)(2,1)}), bf16[8,512,128]{2,1,0:T(8,128)(2,1)S(1)}, u32[]{:S(2)}, u32[]{:S(2)}) async-start(bf16[8,512,128]{2,1,0:T(8,128)(2,1)} %broadcast_in_dim.2), calls=%async_computation | async-start | bytes 2097152 | tf_op jit(solution)/shard_map/all_to_all | solution.py:165
  36.1 9.0 %collective-permute-start.5 = (bf16[2,528,128]{2,1,0:T(8,128)(2,1)}, bf16[2,528,128]{2,1,0:T(8,128)(2,1)S(1)}, u32[]{:S(2)}, u32[]{:S(2)}) collective-permute-start(bf16[2,528,128]{2,1,0:T(8,128)(2,1)} %collective-permute-done.4.refs_5_), channel_id=1, source_target_pairs={{0,64},{8,456},{64,128},{72,8},{128,192},{136,72},{192,256},{200,1... | collective-permute-start | bytes 811016 | tf_op jit(solution)/shard_map/ppermute | solution.py:173
  38.3 1.5 %copy-start = (bf16[528,1152]{1,0:T(8,128)(2,1)}, bf16[528,1152]{1,0:T(8,128)(2,1)S(1)}, u32[]{:S(2)}) copy-start(bf16[528,1152]{1,0:T(8,128)(2,1)S(1)} %collective-permute-done.1.refs_3_) | copy-start | bytes 3649540
  38.4 1.8 %copy-start.1 = (bf16[528,1152]{1,0:T(8,128)(2,1)}, bf16[528,1152]{1,0:T(8,128)(2,1)S(1)}, u32[]{:S(2)}) copy-start(bf16[528,1152]{1,0:T(8,128)(2,1)S(1)} %collective-permute-done.refs_1_) | copy-start | bytes 3649540
  40.1 27.8 %copy-start.8 = (s32[1,8,8]{2,1,0:T(8,128)S(1)}, s32[1,8,8]{2,1,0:T(8,128)}, u32[]{:S(2)}) copy-start(s32[1,8,8]{2,1,0:T(8,128)} %param.10) | copy-start | bytes 772
  40.1 31.6 %collective-permute-start.2 = (bf16[528,1152]{1,0:T(8,128)(2,1)}, bf16[528,1152]{1,0:T(8,128)(2,1)}, u32[]{:S(2)}, u32[]{:S(2)}) collective-permute-start(bf16[528,1152]{1,0:T(8,128)(2,1)} %broadcast_select_fusion), channel_id=1, source_target_pairs={{0,16},{8,56},{16,32},{24,8},{32,48},{40,24},{48,0},{56,40},{1,17}... | collective-permute-start | bytes 3649544 | tf_op jit(solution)/shard_map/ppermute | solution.py:177
  45.1 12.9 %copy-start.4 = (bf16[2,528,128]{2,1,0:T(8,128)(2,1)}, bf16[2,528,128]{2,1,0:T(8,128)(2,1)S(1)}, u32[]{:S(2)}) copy-start(bf16[2,528,128]{2,1,0:T(8,128)(2,1)S(1)} %collective-permute-done.5.refs_6_) | copy-start | bytes 811012
  45.1 12.8 %collective-permute-start.6 = (bf16[2,528,128]{2,1,0:T(8,128)(2,1)S(1)}, bf16[2,528,128]{2,1,0:T(8,128)(2,1)S(1)}, u32[]{:S(2)}, u32[]{:S(2)}) collective-permute-start(bf16[2,528,128]{2,1,0:T(8,128)(2,1)S(1)} %collective-permute-done.5.refs_6_), channel_id=1, source_target_pairs={{0,64},{8,456},{64,128},{72,8},{128,192},{136,72},{192,256},{200,1... | collective-permute-start | bytes 811016 | tf_op jit(solution)/shard_map/ppermute | solution.py:174
  58.0 13.8 %copy-start.5 = (bf16[2,528,128]{2,1,0:T(8,128)(2,1)}, bf16[2,528,128]{2,1,0:T(8,128)(2,1)S(1)}, u32[]{:S(2)}) copy-start(bf16[2,528,128]{2,1,0:T(8,128)(2,1)S(1)} %collective-permute-done.6.refs_7_) | copy-start | bytes 811012
  59.1 12.6 %collective-permute-start.8 = (bf16[3,2,528,128]{3,2,1,0:T(8,128)(2,1)S(1)}, bf16[3,2,528,128]{3,2,1,0:T(8,128)(2,1)S(1)}, u32[]{:S(2)}, u32[]{:S(2)}) collective-permute-start(bf16[3,2,528,128]{3,2,1,0:T(8,128)(2,1)S(1)} %pad_maximum_fusion), channel_id=1, source_target_pairs={{0,8},{8,0},{1,9},{9,1},{2,10},{10,2},{3,11},{11,3},{4,12},{12,4},... | collective-permute-start | bytes 2433032 | tf_op jit(solution)/shard_map/ppermute | solution.py:146
  64.2 7.5 %collective-permute-start.7 = (bf16[2,528,128]{2,1,0:T(8,128)(2,1)S(1)}, bf16[2,528,128]{2,1,0:T(8,128)(2,1)S(1)}, u32[]{:S(2)}, u32[]{:S(2)}) collective-permute-start(bf16[2,528,128]{2,1,0:T(8,128)(2,1)S(1)} %collective-permute-done.6.refs_7_), channel_id=1, source_target_pairs={{0,64},{8,456},{64,128},{72,8},{128,192},{136,72},{192,256},{200,1... | collective-permute-start | bytes 811016 | tf_op jit(solution)/shard_map/ppermute | solution.py:175
  71.7 0.7 copy-start.6
  71.7 1.0 copy-start.3
  71.7 1.3 copy-start.2
  83.9 17.9 %collective-permute-start.9 = (bf16[4,4,2,128,128]{4,3,2,1,0:T(8,128)(2,1)}, bf16[4,4,2,128,128]{4,3,2,1,0:T(8,128)(2,1)S(1)}, u32[]{:S(2)}, u32[]{:S(2)}) collective-permute-start(bf16[4,4,2,128,128]{4,3,2,1,0:T(8,128)(2,1)} %terms.3), channel_id=1, source_target_pairs={{0,1},{1,0},{2,3},{3,2},{4,5},{5,4},{6,7},{7,6},{8,15},{9,10},{10,... | collective-permute-start | bytes 3145736 | tf_op jit(solution)/shard_map/ppermute | solution.py:213

commit v3 on v2

--- a/solution.py
+++ b/solution.py
@@ -14,7 +14,7 @@
 PROWS = RB * BS
 ROWS = PROWS + PAD
 AW = SA * BS + CW
-UNROLL = 4
+UNROLL = 8
 OFF = 255
 FLAG = 20
 BF16, F32, I32 = jnp.bfloat16, jnp.float32, jnp.int32
@@ -24,9 +24,9 @@
     own_ref[:PROWS, : SA * BS] = a_ref[...]
     own_ref[:PROWS, SA * BS :] = p_ref[...]
     message_ref[:PROWS, :] = p_ref[...]
-    listed = jnp.concatenate([lists[z] for z in range(NZ)], 1)
-    listed = jnp.concatenate([listed, jnp.zeros((NX * NC, CW - NZ * GP), I32)], 1)
-    message_ref[PROWS:, :] = jnp.concatenate([listed, jnp.zeros_like(listed)], 0).astype(F32).astype(BF16)
+    message_ref[PROWS:, :] = jnp.zeros((PAD, CW), BF16)
+    listed = jnp.concatenate([lists[...], jnp.zeros((PAD - GP, NZ * NX * NC), I32)], 0)
+    message_ref[PROWS:, : NZ * NX * NC] = listed.astype(F32).astype(BF16)
     entry = cols[...] - NEAR
     far = (entry >= 0) & (lax.broadcasted_iota(I32, (RB, SA), 0) < live[0])
     entry = jnp.where(far, entry, 0)
@@ -83,26 +83,28 @@
                 left[(turn * RB + n) * (SA // 2) + pair] = product[:, pair * CW : (pair + 1) * CW]
     for copy in tables:
         copy.wait()
-    both = p_ref[:, :, pl.ds(PROWS, PAD), :].astype(F32)[:, :, : NX * NC].astype(I32)
-    sent_v[...] = jnp.where(my_c == 0, both[:, :, :NX], both[:, :, NX:]).reshape(NZ, NC * NX, CW)
+    both = p_ref[:, :, pl.ds(PROWS, PAD), :].astype(F32)[:, :, :RB].astype(I32)
+    sent_v[...] = both[:, 0] | (both[:, 1] << 3)
     list_move.start()
 
-    def add_terms(first, turns, block_of, panel_of):
+    def select(first, turns, start):
         def pick(at, count):
             for s in range(SA):
                 item = items[first + (at >> 3), at & 7, s]
-                todo[count] = item
+                todo[start + count] = item
                 count = count + (item >> FLAG)
             return count
 
         count = lax.fori_loop(0, turns * RB, pick, 0)
         for u in range(UNROLL):
-            todo[count + u] = 0
-
+            todo[start + count + u] = 0
+        return count
+
+    def add_terms(start, count, turns, block_of, panel_of):
         def body(step, unused):
             found = []
             for u in range(UNROLL):
-                item = todo[step * UNROLL + u]
+                item = todo[start + step * UNROLL + u]
                 slot = item & (SLOTS * turns - 1)
                 block = block_of(item)
                 odd = (slot & 1) == 1
@@ -126,16 +128,21 @@
     def far_block(item):
         panel = (item >> 12) & 15
         group = (my_x - ((item >> 7) & 3)) & (NX - 1)
-        row = sent[panel >> 1, (panel & 1) * NX + group, my_z * GP + ((item >> 9) & 7)]
+        row = (sent[panel >> 1, (item >> 9) & 7, (my_z * NX + group) * NC + my_c] >> ((panel & 1) * 3)) & 7
         return p_ref[panel >> 1, panel & 1, pl.ds(pl.multiple_of(row * BS, BS), BS), :]
 
+    for move in moves:
+        move.wait()
+    near_start = NX * SLOTS + UNROLL
+    near_count = select(NX, 1, near_start)
+    far_count = select(0, NX, 0)
     near_copy.wait()
-    moves[NX].wait()
-    add_terms(NX, 1, near_block, lambda item: (my_z >> 1) * NC + my_c)
-    for turn in range(NX):
-        moves[turn].wait()
+    add_terms(near_start, near_count, 1, near_block, lambda item: (my_z >> 1) * NC + my_c)
     list_move.wait()
-    add_terms(0, NX, far_block, lambda item: ((item >> 7) & 3) * NZ + ((item >> 14) & 3) * NC + ((item >> 12) & 1))
+    add_terms(
+        0, far_count, NX, far_block,
+        lambda item: ((item >> 7) & 3) * NZ + ((item >> 14) & 3) * NC + ((item >> 12) & 1),
+    )
     for turn in range(NX):
         group = (my_x - turn) & (NX - 1)
         for at in range(NZ):
@@ -151,14 +158,13 @@
     own_p = p_blocks.reshape(PROWS, CW)
     hbm, vmem, smem = (pl.BlockSpec(memory_space=space) for space in (pl.ANY, pltpu.VMEM, pltpu.SMEM))
 
-    by_core = row_send.reshape(NZ, NX, NC, GP).transpose(0, 2, 1, 3).reshape(NZ, NC * NX, GP)
     own, message = pl.pallas_call(
         pack_kernel,
         out_shape=(jax.ShapeDtypeStruct((ROWS, AW), BF16), jax.ShapeDtypeStruct((ROWS, CW), BF16)),
         in_specs=[smem, vmem, vmem, vmem, vmem],
         out_specs=(vmem, vmem),
         name="pack",
-    )(a_live, a_blocks.reshape(PROWS, SA * BS), own_p, a_cols, by_core)
+    )(a_live, a_blocks.reshape(PROWS, SA * BS), own_p, a_cols, row_send[0].T)
 
     low = hop(own, "x", NX, 1)
     high = hop(own, "x", NX, -1)
@@ -196,7 +202,7 @@
                 pltpu.VMEM((NZ, NC * NX, CW), I32),
                 pltpu.SMEM((NX + 1, RB, CW), I32),
                 pltpu.SMEM((NZ, NC * NX, CW), I32),
-                pltpu.SMEM((NX * SLOTS + UNROLL,), I32),
+                pltpu.SMEM(((NX + 1) * SLOTS + 2 * UNROLL,), I32),
                 pltpu.SemaphoreType.DMA((2 * NX + NZ + 3,)),
             ],
             compiler_params=pltpu.CompilerParams(vmem_limit_bytes=56 * 1024 * 1024),

time: 141 us -> 141 us (level)
  transfers between devices with their start and end apart: 11 -> 11, of which waited for: 4 -> 4; matrix products, arithmetic and copies ran while one was open for 5% -> 5% of each run, Pallas kernels for 8% -> 7%
where the time goes in v3:
time: 141 us; the launch traced here: 140 us
  starting transfers between devices  58.7 us (42%)
  blocking collectives  37 us (26%)
  Pallas kernels  22.8 us (16%)
  waiting for transfers between devices  8.47 us (6%)
  other arithmetic  6.66 us (5%)
  local copies, waits for them, and re-layouts  5.96 us (4%)
    all_to_all x1, blocking collectives, shards(): lax.all_to_all(partial.reshape(NX * NY // 2, NC, CW, CW), ('x', 'yh'), sp...  37 us
    pallas_call x2, Pallas kernels, terms(): pl.pallas_call(terms_kernel, out_shape=jax.ShapeDtypeStruct((NX, NZ // 2,...  20.2 us
    ppermute x4, starting transfers between devices, hop(): lax.ppermute(array, axis, [(i, (i + step) % size) for i in range(size)])  19.7 us
    ppermute x1, starting transfers between devices, shards(): three = lax.ppermute(two, ('z', 'c'), around)  9.45 us
    all_to_all x1, starting transfers between devices, shards(): lax.all_to_all(jnp.broadcast_to(own_p[None], (NY, PROWS, CW)), ('yh', 'yl...  6.82 us
    ppermute x1, starting transfers between devices, shards(): one = lax.ppermute(here, ('z', 'c'), around)  6.03 us
    ppermute x1, starting transfers between devices, shards(): given = lax.ppermute(terms(1 - (my_y & 1)), ('c', 'yh', 'yl'), pairs)  5.83 us
    ppermute x1, starting transfers between devices, shards(): lax.ppermute(jnp.where(my_c == 0, low, high), ('x', 'c'), [(x * NC + c, (...  4.97 us
  transfers between devices with their start and end apart: 11, of which 4 were waited for; matrix products, arithmetic and copies ran while one was open for 5% of the time, Pallas kernels for 7%

profile of v3, /device:TPU:1, one launch (start us, length us, event | category | flops | bytes accessed | tf_op | source)
XLA Modules:
  0.0 140.4 jit_solution(11553341287923417758)
XLA Ops:
  0.0 0.0 copy-start.7
  0.7 1.3 copy.9
  2.0 2.5 %pack.1 = (bf16[528,1152]{1,0:T(8,128)(2,1)}, bf16[528,128]{1,0:T(8,128)(2,1)}) custom-call(s32[1]{0:T(128)S(6)} %copy.10.live, bf16[512,1024]{1,0:T(8,128)(2,1)} %bitcast.25, bf16[512,128]{1,0:T(8,128)(2,1)} %bitcast.26, s32[8,16]{1,0:T(8,128)} %cols.5, s32[6,64]{1,0:T(8,128)} %bitcast.30), custom_call_target="tpu_custom_call" | custom-call | tf_op jit(solution)/shard_map/pack/pallas_call | solution.py:161
  4.5 5.2 %collective-permute-start.1 = (bf16[528,1152]{1,0:T(8,128)(2,1)}, bf16[528,1152]{1,0:T(8,128)(2,1)S(1)}, u32[]{:S(2)}, u32[]{:S(2)}) collective-permute-start(bf16[528,1152]{1,0:T(8,128)(2,1)} %get-tuple-element.7.refs_0_), channel_id=1, source_target_pairs={{0,48},{16,0},{32,16},{48,32},{1,49},{17,1},{33,17},{49,33},{2,50}... | collective-permute-start | bytes 3649544 | tf_op jit(solution)/shard_map/ppermute | solution.py:153
  9.7 1.9 %collective-permute-start = (bf16[528,1152]{1,0:T(8,128)(2,1)}, bf16[528,1152]{1,0:T(8,128)(2,1)S(1)}, u32[]{:S(2)}, u32[]{:S(2)}) collective-permute-start(bf16[528,1152]{1,0:T(8,128)(2,1)} %get-tuple-element.7.refs_0_), channel_id=1, source_target_pairs={{0,16},{16,32},{32,48},{48,0},{1,17},{17,33},{33,49},{49,1},{2,18}... | collective-permute-start | bytes 3649544 | tf_op jit(solution)/shard_map/ppermute | solution.py:153
  11.6 7.5 %collective-permute-start.3 = (bf16[528,128]{1,0:T(8,128)(2,1)}, bf16[528,128]{1,0:T(8,128)(2,1)S(1)}, u32[]{:S(2)}, u32[]{:S(2)}) collective-permute-start(bf16[528,128]{1,0:T(8,128)(2,1)} %get-tuple-element.8), channel_id=1, source_target_pairs={{0,8},{8,0},{1,9},{9,1},{2,10},{10,2},{3,11},{11,3},{4,12},{12,4},... | collective-permute-start | bytes 405512 | tf_op jit(solution)/shard_map/ppermute | solution.py:153
  19.1 1.2 collective-permute-done.3
  20.3 1.7 %maximum_select_fusion.refs_4_ = bf16[2,528,128]{2,1,0:T(8,128)(2,1)} fusion(bf16[1,528,128]{2,1,0:T(8,128)(2,1)S(1)} %bitcast.29, bf16[1,528,128]{2,1,0:T(8,128)(2,1)} %bitcast.28, pred[]{:T(512)S(6)} %eq.4), kind=kLoop, calls=%fused_computation.4 | loop fusion | flops 405504 | bytes 540673 | tf_op jit(solution)/shard_map/jit(_where)/select_n | solution.py:177
  22.0 6.0 %collective-permute-start.4 = (bf16[2,528,128]{2,1,0:T(8,128)(2,1)}, bf16[2,528,128]{2,1,0:T(8,128)(2,1)}, u32[]{:S(2)}, u32[]{:S(2)}) collective-permute-start(bf16[2,528,128]{2,1,0:T(8,128)(2,1)} %maximum_select_fusion.refs_4_), channel_id=1, source_target_pairs={{0,64},{8,456},{64,128},{72,8},{128,192},{136,72},{192,256},{200,1... | collective-permute-start | bytes 811016 | tf_op jit(solution)/shard_map/ppermute | solution.py:178
  28.1 0.0 copy-done.7
  28.1 1.1 broadcast_in_dim.2
  29.2 6.8 %all-to-all-start = ((bf16[8,512,128]{2,1,0:T(8,128)(2,1)}), bf16[8,512,128]{2,1,0:T(8,128)(2,1)S(1)}, u32[]{:S(2)}, u32[]{:S(2)}) async-start(bf16[8,512,128]{2,1,0:T(8,128)(2,1)} %broadcast_in_dim.2), calls=%async_computation | async-start | bytes 2097152 | tf_op jit(solution)/shard_map/all_to_all | solution.py:171
  36.0 0.0 collective-permute-done.4.refs_5_
  36.0 2.2 %collective-permute-start.5 = (bf16[2,528,128]{2,1,0:T(8,128)(2,1)}, bf16[2,528,128]{2,1,0:T(8,128)(2,1)S(1)}, u32[]{:S(2)}, u32[]{:S(2)}) collective-permute-start(bf16[2,528,128]{2,1,0:T(8,128)(2,1)} %collective-permute-done.4.refs_5_), channel_id=1, source_target_pairs={{0,64},{8,456},{64,128},{72,8},{128,192},{136,72},{192,256},{200,1... | collective-permute-start | bytes 811016 | tf_op jit(solution)/shard_map/ppermute | solution.py:179
  38.3 0.0 collective-permute-done.1.refs_3_
  38.3 0.0 copy-start
  38.3 0.0 collective-permute-done.refs_1_
  38.3 0.0 copy-start.1
  38.3 1.3 broadcast_select_fusion
  39.6 0.1 copy-done
  39.7 0.3 copy-done.1
  40.0 0.0 copy-start.8
  40.0 5.0 %collective-permute-start.2 = (bf16[528,1152]{1,0:T(8,128)(2,1)}, bf16[528,1152]{1,0:T(8,128)(2,1)}, u32[]{:S(2)}, u32[]{:S(2)}) collective-permute-start(bf16[528,1152]{1,0:T(8,128)(2,1)} %broadcast_select_fusion), channel_id=1, source_target_pairs={{0,16},{8,56},{16,32},{24,8},{32,48},{40,24},{48,0},{56,40},{1,17}... | collective-permute-start | bytes 3649544 | tf_op jit(solution)/shard_map/ppermute | solution.py:183
  45.0 0.0 collective-permute-done.5.refs_6_
  45.0 0.0 copy-start.4
  45.0 9.5 %collective-permute-start.6 = (bf16[2,528,128]{2,1,0:T(8,128)(2,1)S(1)}, bf16[2,528,128]{2,1,0:T(8,128)(2,1)S(1)}, u32[]{:S(2)}, u32[]{:S(2)}) collective-permute-start(bf16[2,528,128]{2,1,0:T(8,128)(2,1)S(1)} %collective-permute-done.5.refs_6_), channel_id=1, source_target_pairs={{0,64},{8,456},{64,128},{72,8},{128,192},{136,72},{192,256},{200,1... | collective-permute-start | bytes 811016 | tf_op jit(solution)/shard_map/ppermute | solution.py:180
  54.5 3.4 %collective-permute-done.6.refs_7_ = bf16[2,528,128]{2,1,0:T(8,128)(2,1)S(1)} collective-permute-done((bf16[2,528,128]{2,1,0:T(8,128)(2,1)S(1)}, bf16[2,528,128]{2,1,0:T(8,128)(2,1)S(1)}, u32[]{:S(2)}, u32[]{:S(2)}) %collective-permute-start.6) | collective-permute-done | bytes 270368 | tf_op jit(solution)/shard_map/ppermute | solution.py:180
  57.9 0.0 copy-start.5
  57.9 0.0 copy-done.4
  57.9 1.1 pad_maximum_fusion
  59.0 5.1 %collective-permute-start.8 = (bf16[3,2,528,128]{3,2,1,0:T(8,128)(2,1)S(1)}, bf16[3,2,528,128]{3,2,1,0:T(8,128)(2,1)S(1)}, u32[]{:S(2)}, u32[]{:S(2)}) collective-permute-start(bf16[3,2,528,128]{3,2,1,0:T(8,128)(2,1)S(1)} %pad_maximum_fusion), channel_id=1, source_target_pairs={{0,8},{8,0},{1,9},{9,1},{2,10},{10,2},{3,11},{11,3},{4,12},{12,4},... | collective-permute-start | bytes 2433032 | tf_op jit(solution)/shard_map/ppermute | solution.py:153
  64.1 3.6 %collective-permute-start.7 = (bf16[2,528,128]{2,1,0:T(8,128)(2,1)S(1)}, bf16[2,528,128]{2,1,0:T(8,128)(2,1)S(1)}, u32[]{:S(2)}, u32[]{:S(2)}) collective-permute-start(bf16[2,528,128]{2,1,0:T(8,128)(2,1)S(1)} %collective-permute-done.6.refs_7_), channel_id=1, source_target_pairs={{0,64},{8,456},{64,128},{72,8},{128,192},{136,72},{192,256},{200,1... | collective-permute-start | bytes 811016 | tf_op jit(solution)/shard_map/ppermute | solution.py:181
  67.8 0.0 copy-done.8
  67.8 0.6 reshape.20.need
  68.4 0.6 stack.69.place
  69.0 2.6 %collective-permute-done.7.refs_8_ = bf16[2,528,128]{2,1,0:T(8,128)(2,1)S(1)} collective-permute-done((bf16[2,528,128]{2,1,0:T(8,128)(2,1)S(1)}, bf16[2,528,128]{2,1,0:T(8,128)(2,1)S(1)}, u32[]{:S(2)}, u32[]{:S(2)}) %collective-permute-start.7) | collective-permute-done | bytes 270368 | tf_op jit(solution)/shard_map/ppermute | solution.py:181
  71.6 0.0 copy-start.6
  71.6 0.0 collective-permute-done.8.refs_9_
  71.6 0.0 copy-start.3
  71.7 0.0 all-to-all-done.refs_10_
  71.7 0.0 copy-start.2
  71.7 0.0 collective-permute-done.2.refs_2_
  71.7 0.0 copy-done.5
  71.7 0.7 copy-done.6
  72.4 0.3 copy-done.3
  72.7 0.3 copy-done.2
  73.0 9.7 %terms.3 = bf16[4,4,2,128,128]{4,3,2,1,0:T(8,128)(2,1)} custom-call(s32[6]{0:T(128)} %stack.69.place, s32[64]{0:T(128)} %reshape.20.need, s32[8,16]{1,0:T(8,128)} %cols.5, bf16[528,1152]{1,0:T(8,128)(2,1)} %get-tuple-element.7.refs_0_, bf16[528,1152]{1,0:T(8,128)(2,1)} %copy-done.1, bf16[528,1152]{1,0:T(8,128)(2,1)} %collective-permute-done.2.refs_2_, ...), custom_call_target="tpu_custom_call" | custom-call | flops 2000000000 | bytes 12000000 | tf_op jit(solution)/shard_map/terms/pallas_call | solution.py:190
  82.7 5.8 %collective-permute-start.9 = (bf16[4,4,2,128,128]{4,3,2,1,0:T(8,128)(2,1)}, bf16[4,4,2,128,128]{4,3,2,1,0:T(8,128)(2,1)S(1)}, u32[]{:S(2)}, u32[]{:S(2)}) collective-permute-start(bf16[4,4,2,128,128]{4,3,2,1,0:T(8,128)(2,1)} %terms.3), channel_id=1, source_target_pairs={{0,1},{1,0},{2,3},{3,2},{4,5},{5,4},{6,7},{7,6},{8,15},{9,10},{10,... | collective-permute-start | bytes 3145736 | tf_op jit(solution)/shard_map/ppermute | solution.py:219
  88.6 0.6 stack.59.place
  89.2 10.5 %terms.2 = bf16[4,4,2,128,128]{4,3,2,1,0:T(8,128)(2,1)} custom-call(s32[6]{0:T(128)} %stack.59.place, s32[64]{0:T(128)} %reshape.20.need, s32[8,16]{1,0:T(8,128)} %cols.5, bf16[528,1152]{1,0:T(8,128)(2,1)} %get-tuple-element.7.refs_0_, bf16[528,1152]{1,0:T(8,128)(2,1)} %copy-done.1, bf16[528,1152]{1,0:T(8,128)(2,1)} %collective-permute-done.2.refs_2_, ...), custom_call_target="tpu_custom_call" | custom-call | flops 2000000000 | bytes 12000000 | tf_op jit(solution)/shard_map/terms/pallas_call | solution.py:190
  99.7 1.3 collective-permute-done.9
  101.0 1.6 %add_convert_fusion = bf16[4,4,2,128,128]{4,3,2,1,0:T(8,128)(2,1)S(1)} fusion(bf16[4,4,2,128,128]{4,3,2,1,0:T(8,128)(2,1)S(1)} %collective-permute-done.9, bf16[4,4,2,128,128]{4,3,2,1,0:T(8,128)(2,1)} %terms.2), kind=kLoop, calls=%fused_computation | loop fusion | flops 2097152 | bytes 3145728 | tf_op jit(solution)/shard_map/convert_element_type | solution.py:221
  102.6 37.0 %all_to_all.10 = bf16[16,2,128,128]{3,2,1,0:T(8,128)(2,1)S(1)} all-to-all(bf16[16,2,128,128]{3,2,1,0:T(8,128)(2,1)S(1)} %bitcast.22), channel_id=1, replica_groups=mesh['z'=8,'x'=4,'c'=2,'yh'=4,'yl'=2] {'x','yh'}, dimensions={0} | all-to-all | bytes 2097152 | tf_op jit(solution)/shard_map/all_to_all | solution.py:223
  139.6 0.9 bitcast_reduce_fusion
Async XLA Ops:
  0.0 28.1 %copy-start.7 = (bf16[8,64,128]{2,1,0:T(8,128)(2,1)S(1)}, bf16[8,64,128]{2,1,0:T(8,128)(2,1)}, u32[]{:S(2)}) copy-start(bf16[8,64,128]{2,1,0:T(8,128)(2,1)} %param.7) | copy-start | bytes 393220
  4.5 33.8 %collective-permute-start.1 = (bf16[528,1152]{1,0:T(8,128)(2,1)}, bf16[528,1152]{1,0:T(8,128)(2,1)S(1)}, u32[]{:S(2)}, u32[]{:S(2)}) collective-permute-start(bf16[528,1152]{1,0:T(8,128)(2,1)} %get-tuple-element.7.refs_0_), channel_id=1, source_target_pairs={{0,48},{16,0},{32,16},{48,32},{1,49},{17,1},{33,17},{49,33},{2,50}... | collective-permute-start | bytes 3649544 | tf_op jit(solution)/shard_map/ppermute | solution.py:153
  9.7 28.6 %collective-permute-start = (bf16[528,1152]{1,0:T(8,128)(2,1)}, bf16[528,1152]{1,0:T(8,128)(2,1)S(1)}, u32[]{:S(2)}, u32[]{:S(2)}) collective-permute-start(bf16[528,1152]{1,0:T(8,128)(2,1)} %get-tuple-element.7.refs_0_), channel_id=1, source_target_pairs={{0,16},{16,32},{32,48},{48,0},{1,17},{17,33},{33,49},{49,1},{2,18}... | collective-permute-start | bytes 3649544 | tf_op jit(solution)/shard_map/ppermute | solution.py:153
  11.6 8.7 %collective-permute-start.3 = (bf16[528,128]{1,0:T(8,128)(2,1)}, bf16[528,128]{1,0:T(8,128)(2,1)S(1)}, u32[]{:S(2)}, u32[]{:S(2)}) collective-permute-start(bf16[528,128]{1,0:T(8,128)(2,1)} %get-tuple-element.8), channel_id=1, source_target_pairs={{0,8},{8,0},{1,9},{9,1},{2,10},{10,2},{3,11},{11,3},{4,12},{12,4},... | collective-permute-start | bytes 405512 | tf_op jit(solution)/shard_map/ppermute | solution.py:153
  22.0 14.0 %collective-permute-start.4 = (bf16[2,528,128]{2,1,0:T(8,128)(2,1)}, bf16[2,528,128]{2,1,0:T(8,128)(2,1)}, u32[]{:S(2)}, u32[]{:S(2)}) collective-permute-start(bf16[2,528,128]{2,1,0:T(8,128)(2,1)} %maximum_select_fusion.refs_4_), channel_id=1, source_target_pairs={{0,64},{8,456},{64,128},{72,8},{128,192},{136,72},{192,256},{200,1... | collective-permute-start | bytes 811016 | tf_op jit(solution)/shard_map/ppermute | solution.py:178
  29.2 42.4 %all-to-all-start = ((bf16[8,512,128]{2,1,0:T(8,128)(2,1)}), bf16[8,512,128]{2,1,0:T(8,128)(2,1)S(1)}, u32[]{:S(2)}, u32[]{:S(2)}) async-start(bf16[8,512,128]{2,1,0:T(8,128)(2,1)} %broadcast_in_dim.2), calls=%async_computation | async-start | bytes 2097152 | tf_op jit(solution)/shard_map/all_to_all | solution.py:171
  36.0 9.0 %collective-permute-start.5 = (bf16[2,528,128]{2,1,0:T(8,128)(2,1)}, bf16[2,528,128]{2,1,0:T(8,128)(2,1)S(1)}, u32[]{:S(2)}, u32[]{:S(2)}) collective-permute-start(bf16[2,528,128]{2,1,0:T(8,128)(2,1)} %collective-permute-done.4.refs_5_), channel_id=1, source_target_pairs={{0,64},{8,456},{64,128},{72,8},{128,192},{136,72},{192,256},{200,1... | collective-permute-start | bytes 811016 | tf_op jit(solution)/shard_map/ppermute | solution.py:179
  38.3 1.5 %copy-start = (bf16[528,1152]{1,0:T(8,128)(2,1)}, bf16[528,1152]{1,0:T(8,128)(2,1)S(1)}, u32[]{:S(2)}) copy-start(bf16[528,1152]{1,0:T(8,128)(2,1)S(1)} %collective-permute-done.1.refs_3_) | copy-start | bytes 3649540
  38.3 1.8 %copy-start.1 = (bf16[528,1152]{1,0:T(8,128)(2,1)}, bf16[528,1152]{1,0:T(8,128)(2,1)S(1)}, u32[]{:S(2)}) copy-start(bf16[528,1152]{1,0:T(8,128)(2,1)S(1)} %collective-permute-done.refs_1_) | copy-start | bytes 3649540
  40.0 27.8 %copy-start.8 = (s32[1,8,8]{2,1,0:T(8,128)S(1)}, s32[1,8,8]{2,1,0:T(8,128)}, u32[]{:S(2)}) copy-start(s32[1,8,8]{2,1,0:T(8,128)} %param.10) | copy-start | bytes 772
  40.0 31.6 %collective-permute-start.2 = (bf16[528,1152]{1,0:T(8,128)(2,1)}, bf16[528,1152]{1,0:T(8,128)(2,1)}, u32[]{:S(2)}, u32[]{:S(2)}) collective-permute-start(bf16[528,1152]{1,0:T(8,128)(2,1)} %broadcast_select_fusion), channel_id=1, source_target_pairs={{0,16},{8,56},{16,32},{24,8},{32,48},{40,24},{48,0},{56,40},{1,17}... | collective-permute-start | bytes 3649544 | tf_op jit(solution)/shard_map/ppermute | solution.py:183
  45.0 12.9 %copy-start.4 = (bf16[2,528,128]{2,1,0:T(8,128)(2,1)}, bf16[2,528,128]{2,1,0:T(8,128)(2,1)S(1)}, u32[]{:S(2)}) copy-start(bf16[2,528,128]{2,1,0:T(8,128)(2,1)S(1)} %collective-permute-done.5.refs_6_) | copy-start | bytes 811012
  45.0 12.8 %collective-permute-start.6 = (bf16[2,528,128]{2,1,0:T(8,128)(2,1)S(1)}, bf16[2,528,128]{2,1,0:T(8,128)(2,1)S(1)}, u32[]{:S(2)}, u32[]{:S(2)}) collective-permute-start(bf16[2,528,128]{2,1,0:T(8,128)(2,1)S(1)} %collective-permute-done.5.refs_6_), channel_id=1, source_target_pairs={{0,64},{8,456},{64,128},{72,8},{128,192},{136,72},{192,256},{200,1... | collective-permute-start | bytes 811016 | tf_op jit(solution)/shard_map/ppermute | solution.py:180
  57.9 13.8 %copy-start.5 = (bf16[2,528,128]{2,1,0:T(8,128)(2,1)}, bf16[2,528,128]{2,1,0:T(8,128)(2,1)S(1)}, u32[]{:S(2)}) copy-start(bf16[2,528,128]{2,1,0:T(8,128)(2,1)S(1)} %collective-permute-done.6.refs_7_) | copy-start | bytes 811012
  59.0 12.6 %collective-permute-start.8 = (bf16[3,2,528,128]{3,2,1,0:T(8,128)(2,1)S(1)}, bf16[3,2,528,128]{3,2,1,0:T(8,128)(2,1)S(1)}, u32[]{:S(2)}, u32[]{:S(2)}) collective-permute-start(bf16[3,2,528,128]{3,2,1,0:T(8,128)(2,1)S(1)} %pad_maximum_fusion), channel_id=1, source_target_pairs={{0,8},{8,0},{1,9},{9,1},{2,10},{10,2},{3,11},{11,3},{4,12},{12,4},... | collective-permute-start | bytes 2433032 | tf_op jit(solution)/shard_map/ppermute | solution.py:153
  64.1 7.5 %collective-permute-start.7 = (bf16[2,528,128]{2,1,0:T(8,128)(2,1)S(1)}, bf16[2,528,128]{2,1,0:T(8,128)(2,1)S(1)}, u32[]{:S(2)}, u32[]{:S(2)}) collective-permute-start(bf16[2,528,128]{2,1,0:T(8,128)(2,1)S(1)} %collective-permute-done.6.refs_7_), channel_id=1, source_target_pairs={{0,64},{8,456},{64,128},{72,8},{128,192},{136,72},{192,256},{200,1... | collective-permute-start | bytes 811016 | tf_op jit(solution)/shard_map/ppermute | solution.py:181
  71.6 0.7 copy-start.6
  71.6 1.0 copy-start.3
  71.7 1.3 copy-start.2
  82.7 18.2 %collective-permute-start.9 = (bf16[4,4,2,128,128]{4,3,2,1,0:T(8,128)(2,1)}, bf16[4,4,2,128,128]{4,3,2,1,0:T(8,128)(2,1)S(1)}, u32[]{:S(2)}, u32[]{:S(2)}) collective-permute-start(bf16[4,4,2,128,128]{4,3,2,1,0:T(8,128)(2,1)} %terms.3), channel_id=1, source_target_pairs={{0,1},{1,0},{2,3},{3,2},{4,5},{5,4},{6,7},{7,6},{8,15},{9,10},{10,... | collective-permute-start | bytes 3145736 | tf_op jit(solution)/shard_map/ppermute | solution.py:219

commit v4 on v3

--- a/solution.py
+++ b/solution.py
@@ -44,19 +44,20 @@
     back = 2 * my_c - 1
     copies = [pltpu.make_async_copy(groups_hbm[turn], a_ref.at[turn], sems.at[turn]) for turn in range(NX)]
     sources = [(here_hbm, 0), (one_hbm, back), (two_hbm, 2 * back), (three_hbm, 3 * back), (four_hbm, 4)]
-    sources += [(crossed_hbm.at[s], -(s + 1) * back) for s in range(3)]
-    tables = [
-        pltpu.make_async_copy(source, p_ref.at[(my_z + step) & (NZ - 1)], sems.at[NX + at])
-        for at, (source, step) in enumerate(sources)
+    spots = [(source, p_ref.at[(my_z + step) & (NZ - 1)]) for source, step in sources]
+    spots += [
+        (crossed_hbm.at[s, 1 - c], p_ref.at[(my_z - (s + 1) * back) & (NZ - 1), c]) for s in range(3) for c in range(NC)
     ]
-    near_copy = pltpu.make_async_copy(near_hbm, near_ref, sems.at[NX + NZ])
+    tables = [pltpu.make_async_copy(*spot, sems.at[NX + at]) for at, spot in enumerate(spots)]
+    after = NX + len(tables)
+    near_copy = pltpu.make_async_copy(near_hbm, near_ref, sems.at[after])
     for copy in copies[:1] + tables + [near_copy] + copies[1:]:
         copy.start()
     slots = lax.broadcasted_iota(I32, (RB, CW), 0) * SA + lax.broadcasted_iota(I32, (RB, CW), 1)
     moves = [
-        pltpu.make_async_copy(items_v.at[turn], items.at[turn], sems.at[NX + NZ + 1 + turn]) for turn in range(NX + 1)
+        pltpu.make_async_copy(items_v.at[turn], items.at[turn], sems.at[after + 1 + turn]) for turn in range(NX + 1)
     ]
-    list_move = pltpu.make_async_copy(sent_v, sent, sems.at[2 * NX + NZ + 2])
+    list_move = pltpu.make_async_copy(sent_v, sent, sems.at[after + NX + 2])
 
     entry = cols[...]
     close = (entry < NEAR) & (lax.broadcasted_iota(I32, (RB, SA), 0) < live) & ((my_z & 1) == odd_z)
@@ -128,8 +129,9 @@
     def far_block(item):
         panel = (item >> 12) & 15
         group = (my_x - ((item >> 7) & 3)) & (NX - 1)
-        row = (sent[panel >> 1, (item >> 9) & 7, (my_z * NX + group) * NC + my_c] >> ((panel & 1) * 3)) & 7
-        return p_ref[panel >> 1, panel & 1, pl.ds(pl.multiple_of(row * BS, BS), BS), :]
+        other = (panel & 1) ^ my_c
+        row = (sent[panel >> 1, (item >> 9) & 7, (my_z * NX + group) * NC + my_c] >> (other * 3)) & 7
+        return p_ref[panel >> 1, other, pl.ds(pl.multiple_of(row * BS, BS), BS), :]
 
     for move in moves:
         move.wait()
@@ -174,7 +176,7 @@
 
     around = [(z * NC + c, (z + 1 - 2 * c) % NZ * NC + c) for z in range(NZ) for c in range(NC)]
     beside = hop(message, "c", NC, 1)
-    here = jnp.where(my_c == 0, jnp.stack([message, beside]), jnp.stack([beside, message]))
+    here = jnp.stack([message, beside])
     one = lax.ppermute(here, ("z", "c"), around)
     two = lax.ppermute(one, ("z", "c"), around)
     three = lax.ppermute(two, ("z", "c"), around)
@@ -203,7 +205,7 @@
                 pltpu.SMEM((NX + 1, RB, CW), I32),
                 pltpu.SMEM((NZ, NC * NX, CW), I32),
                 pltpu.SMEM(((NX + 1) * SLOTS + 2 * UNROLL,), I32),
-                pltpu.SemaphoreType.DMA((2 * NX + NZ + 3,)),
+                pltpu.SemaphoreType.DMA((2 * NX + NZ + 6,)),
             ],
             compiler_params=pltpu.CompilerParams(vmem_limit_bytes=56 * 1024 * 1024),
             cost_estimate=pl.CostEstimate(flops=2 * 10**9, bytes_accessed=12 * 10**6, transcendentals=0),

time: 141 us -> 141 us (level)
    select_n x1 -> x0, other arithmetic: 1.74 us -> none  [shards(): jnp.where(my_c == 0, jnp.stack([message, beside]), jnp.stack([beside, mes...]
    another operation x0 -> x1, other arithmetic: none -> 1.65 us  [shards(): here = jnp.stack([message, beside])]
where the time goes in v4:
time: 141 us; the launch traced here: 140 us
  starting transfers between devices  58.5 us (41%)
  blocking collectives  36.9 us (26%)
  Pallas kernels  22 us (16%)
  waiting for transfers between devices  9.22 us (7%)
  other arithmetic  6.57 us (5%)
  local copies, waits for them, and re-layouts  5.96 us (4%)
    all_to_all x1, blocking collectives, shards(): lax.all_to_all(partial.reshape(NX * NY // 2, NC, CW, CW), ('x', 'yh'), sp...  36.9 us
    ppermute x4, starting transfers between devices, hop(): lax.ppermute(array, axis, [(i, (i + step) % size) for i in range(size)])  19.7 us
    pallas_call x2, Pallas kernels, terms(): pl.pallas_call(terms_kernel, out_shape=jax.ShapeDtypeStruct((NX, NZ // 2,...  19.5 us
    ppermute x1, starting transfers between devices, shards(): three = lax.ppermute(two, ('z', 'c'), around)  9.54 us
    all_to_all x1, starting transfers between devices, shards(): lax.all_to_all(jnp.broadcast_to(own_p[None], (NY, PROWS, CW)), ('yh', 'yl...  6.82 us
    ppermute x1, starting transfers between devices, shards(): one = lax.ppermute(here, ('z', 'c'), around)  6.03 us
    ppermute x1, starting transfers between devices, shards(): given = lax.ppermute(terms(1 - (my_y & 1)), ('c', 'yh', 'yl'), pairs)  5.59 us
    ppermute x1, starting transfers between devices, shards(): lax.ppermute(jnp.where(my_c == 0, low, high), ('x', 'c'), [(x * NC + c, (...  4.97 us
  transfers between devices with their start and end apart: 11, of which 4 were waited for; matrix products, arithmetic and copies ran while one was open for 5% of the time, Pallas kernels for 7%

profile of v4, /device:TPU:1, one launch (start us, length us, event | category | flops | bytes accessed | tf_op | source)
XLA Modules:
  0.0 140.2 jit_solution(2670019861892188485)
XLA Ops:
  0.0 0.0 copy-start.7
  0.7 1.3 copy.9
  2.0 2.5 %pack.1 = (bf16[528,1152]{1,0:T(8,128)(2,1)}, bf16[528,128]{1,0:T(8,128)(2,1)}) custom-call(s32[1]{0:T(128)S(6)} %copy.10.live, bf16[512,1024]{1,0:T(8,128)(2,1)} %bitcast.25, bf16[512,128]{1,0:T(8,128)(2,1)} %bitcast.26, s32[8,16]{1,0:T(8,128)} %cols.5, s32[6,64]{1,0:T(8,128)} %bitcast.30), custom_call_target="tpu_custom_call" | custom-call | tf_op jit(solution)/shard_map/pack/pallas_call | solution.py:163
  4.5 5.2 %collective-permute-start.1 = (bf16[528,1152]{1,0:T(8,128)(2,1)}, bf16[528,1152]{1,0:T(8,128)(2,1)S(1)}, u32[]{:S(2)}, u32[]{:S(2)}) collective-permute-start(bf16[528,1152]{1,0:T(8,128)(2,1)} %get-tuple-element.7.refs_0_), channel_id=1, source_target_pairs={{0,48},{16,0},{32,16},{48,32},{1,49},{17,1},{33,17},{49,33},{2,50}... | collective-permute-start | bytes 3649544 | tf_op jit(solution)/shard_map/ppermute | solution.py:155
  9.7 1.9 %collective-permute-start = (bf16[528,1152]{1,0:T(8,128)(2,1)}, bf16[528,1152]{1,0:T(8,128)(2,1)S(1)}, u32[]{:S(2)}, u32[]{:S(2)}) collective-permute-start(bf16[528,1152]{1,0:T(8,128)(2,1)} %get-tuple-element.7.refs_0_), channel_id=1, source_target_pairs={{0,16},{16,32},{32,48},{48,0},{1,17},{17,33},{33,49},{49,1},{2,18}... | collective-permute-start | bytes 3649544 | tf_op jit(solution)/shard_map/ppermute | solution.py:155
  11.6 7.5 %collective-permute-start.3 = (bf16[528,128]{1,0:T(8,128)(2,1)}, bf16[528,128]{1,0:T(8,128)(2,1)S(1)}, u32[]{:S(2)}, u32[]{:S(2)}) collective-permute-start(bf16[528,128]{1,0:T(8,128)(2,1)} %get-tuple-element.8), channel_id=1, source_target_pairs={{0,8},{8,0},{1,9},{9,1},{2,10},{10,2},{3,11},{11,3},{4,12},{12,4},... | collective-permute-start | bytes 405512 | tf_op jit(solution)/shard_map/ppermute | solution.py:155
  19.1 1.2 collective-permute-done.3
  20.3 1.7 %pad_maximum_fusion.1.refs_4_ = bf16[2,528,128]{2,1,0:T(8,128)(2,1)} fusion(bf16[1,528,128]{2,1,0:T(8,128)(2,1)S(1)} %bitcast.29, bf16[1,528,128]{2,1,0:T(8,128)(2,1)} %bitcast.28), kind=kLoop, calls=%fused_computation.4 | loop fusion | flops 135168 | bytes 540672 | tf_op jit(solution)/shard_map/stack | solution.py:179
  22.0 6.0 %collective-permute-start.4 = (bf16[2,528,128]{2,1,0:T(8,128)(2,1)}, bf16[2,528,128]{2,1,0:T(8,128)(2,1)}, u32[]{:S(2)}, u32[]{:S(2)}) collective-permute-start(bf16[2,528,128]{2,1,0:T(8,128)(2,1)} %pad_maximum_fusion.1.refs_4_), channel_id=1, source_target_pairs={{0,64},{8,456},{64,128},{72,8},{128,192},{136,72},{192,256},{200,1... | collective-permute-start | bytes 811016 | tf_op jit(solution)/shard_map/ppermute | solution.py:180
  28.0 0.0 copy-done.7
  28.0 1.1 broadcast_in_dim.2
  29.1 6.8 %all-to-all-start = ((bf16[8,512,128]{2,1,0:T(8,128)(2,1)}), bf16[8,512,128]{2,1,0:T(8,128)(2,1)S(1)}, u32[]{:S(2)}, u32[]{:S(2)}) async-start(bf16[8,512,128]{2,1,0:T(8,128)(2,1)} %broadcast_in_dim.2), calls=%async_computation | async-start | bytes 2097152 | tf_op jit(solution)/shard_map/all_to_all | solution.py:173
  36.0 0.0 collective-permute-done.4.refs_5_
  36.0 2.2 %collective-permute-start.5 = (bf16[2,528,128]{2,1,0:T(8,128)(2,1)}, bf16[2,528,128]{2,1,0:T(8,128)(2,1)S(1)}, u32[]{:S(2)}, u32[]{:S(2)}) collective-permute-start(bf16[2,528,128]{2,1,0:T(8,128)(2,1)} %collective-permute-done.4.refs_5_), channel_id=1, source_target_pairs={{0,64},{8,456},{64,128},{72,8},{128,192},{136,72},{192,256},{200,1... | collective-permute-start | bytes 811016 | tf_op jit(solution)/shard_map/ppermute | solution.py:181
  38.2 0.0 collective-permute-done.1.refs_3_
  38.2 0.0 copy-start
  38.2 0.0 collective-permute-done.refs_1_
  38.2 0.0 copy-start.1
  38.2 1.3 broadcast_select_fusion
  39.5 0.1 copy-done
  39.7 0.3 copy-done.1
  40.0 0.0 copy-start.8
  40.0 5.0 %collective-permute-start.2 = (bf16[528,1152]{1,0:T(8,128)(2,1)}, bf16[528,1152]{1,0:T(8,128)(2,1)}, u32[]{:S(2)}, u32[]{:S(2)}) collective-permute-start(bf16[528,1152]{1,0:T(8,128)(2,1)} %broadcast_select_fusion), channel_id=1, source_target_pairs={{0,16},{8,56},{16,32},{24,8},{32,48},{40,24},{48,0},{56,40},{1,17}... | collective-permute-start | bytes 3649544 | tf_op jit(solution)/shard_map/ppermute | solution.py:185
  44.9 0.0 collective-permute-done.5.refs_6_
  45.0 0.0 copy-start.4
  45.0 9.5 %collective-permute-start.6 = (bf16[2,528,128]{2,1,0:T(8,128)(2,1)S(1)}, bf16[2,528,128]{2,1,0:T(8,128)(2,1)S(1)}, u32[]{:S(2)}, u32[]{:S(2)}) collective-permute-start(bf16[2,528,128]{2,1,0:T(8,128)(2,1)S(1)} %collective-permute-done.5.refs_6_), channel_id=1, source_target_pairs={{0,64},{8,456},{64,128},{72,8},{128,192},{136,72},{192,256},{200,1... | collective-permute-start | bytes 811016 | tf_op jit(solution)/shard_map/ppermute | solution.py:182
  54.5 3.4 %collective-permute-done.6.refs_7_ = bf16[2,528,128]{2,1,0:T(8,128)(2,1)S(1)} collective-permute-done((bf16[2,528,128]{2,1,0:T(8,128)(2,1)S(1)}, bf16[2,528,128]{2,1,0:T(8,128)(2,1)S(1)}, u32[]{:S(2)}, u32[]{:S(2)}) %collective-permute-start.6) | collective-permute-done | bytes 270368 | tf_op jit(solution)/shard_map/ppermute | solution.py:182
  57.9 0.0 copy-start.5
  57.9 0.0 copy-done.4
  57.9 1.1 pad_maximum_fusion
  59.0 5.1 %collective-permute-start.8 = (bf16[3,2,528,128]{3,2,1,0:T(8,128)(2,1)S(1)}, bf16[3,2,528,128]{3,2,1,0:T(8,128)(2,1)S(1)}, u32[]{:S(2)}, u32[]{:S(2)}) collective-permute-start(bf16[3,2,528,128]{3,2,1,0:T(8,128)(2,1)S(1)} %pad_maximum_fusion), channel_id=1, source_target_pairs={{0,8},{8,0},{1,9},{9,1},{2,10},{10,2},{3,11},{11,3},{4,12},{12,4},... | collective-permute-start | bytes 2433032 | tf_op jit(solution)/shard_map/ppermute | solution.py:155
  64.1 3.6 %collective-permute-start.7 = (bf16[2,528,128]{2,1,0:T(8,128)(2,1)S(1)}, bf16[2,528,128]{2,1,0:T(8,128)(2,1)S(1)}, u32[]{:S(2)}, u32[]{:S(2)}) collective-permute-start(bf16[2,528,128]{2,1,0:T(8,128)(2,1)S(1)} %collective-permute-done.6.refs_7_), channel_id=1, source_target_pairs={{0,64},{8,456},{64,128},{72,8},{128,192},{136,72},{192,256},{200,1... | collective-permute-start | bytes 811016 | tf_op jit(solution)/shard_map/ppermute | solution.py:183
  67.8 0.0 copy-done.8
  67.8 0.6 reshape.20.need
  68.4 0.6 stack.63.place
  69.0 2.6 %collective-permute-done.7.refs_8_ = bf16[2,528,128]{2,1,0:T(8,128)(2,1)S(1)} collective-permute-done((bf16[2,528,128]{2,1,0:T(8,128)(2,1)S(1)}, bf16[2,528,128]{2,1,0:T(8,128)(2,1)S(1)}, u32[]{:S(2)}, u32[]{:S(2)}) %collective-permute-start.7) | collective-permute-done | bytes 270368 | tf_op jit(solution)/shard_map/ppermute | solution.py:183
  71.6 0.0 copy-start.6
  71.6 0.0 collective-permute-done.8.refs_9_
  71.6 0.0 copy-start.3
  71.7 0.0 all-to-all-done.refs_10_
  71.7 0.0 copy-start.2
  71.7 0.0 collective-permute-done.2.refs_2_
  71.7 0.0 copy-done.5
  71.7 0.7 copy-done.6
  72.4 0.3 copy-done.3
  72.7 0.3 copy-done.2
  73.0 9.8 %terms.3 = bf16[4,4,2,128,128]{4,3,2,1,0:T(8,128)(2,1)} custom-call(s32[6]{0:T(128)} %stack.63.place, s32[64]{0:T(128)} %reshape.20.need, s32[8,16]{1,0:T(8,128)} %cols.5, bf16[528,1152]{1,0:T(8,128)(2,1)} %get-tuple-element.7.refs_0_, bf16[528,1152]{1,0:T(8,128)(2,1)} %copy-done.1, bf16[528,1152]{1,0:T(8,128)(2,1)} %collective-permute-done.2.refs_2_, ...), custom_call_target="tpu_custom_call" | custom-call | flops 2000000000 | bytes 12000000 | tf_op jit(solution)/shard_map/terms/pallas_call | solution.py:192
  82.8 5.6 %collective-permute-start.9 = (bf16[4,4,2,128,128]{4,3,2,1,0:T(8,128)(2,1)}, bf16[4,4,2,128,128]{4,3,2,1,0:T(8,128)(2,1)S(1)}, u32[]{:S(2)}, u32[]{:S(2)}) collective-permute-start(bf16[4,4,2,128,128]{4,3,2,1,0:T(8,128)(2,1)} %terms.3), channel_id=1, source_target_pairs={{0,1},{1,0},{2,3},{3,2},{4,5},{5,4},{6,7},{7,6},{8,15},{9,10},{10,... | collective-permute-start | bytes 3145736 | tf_op jit(solution)/shard_map/ppermute | solution.py:221
  88.4 0.6 stack.54.place
  89.0 9.8 %terms.2 = bf16[4,4,2,128,128]{4,3,2,1,0:T(8,128)(2,1)} custom-call(s32[6]{0:T(128)} %stack.54.place, s32[64]{0:T(128)} %reshape.20.need, s32[8,16]{1,0:T(8,128)} %cols.5, bf16[528,1152]{1,0:T(8,128)(2,1)} %get-tuple-element.7.refs_0_, bf16[528,1152]{1,0:T(8,128)(2,1)} %copy-done.1, bf16[528,1152]{1,0:T(8,128)(2,1)} %collective-permute-done.2.refs_2_, ...), custom_call_target="tpu_custom_call" | custom-call | flops 2000000000 | bytes 12000000 | tf_op jit(solution)/shard_map/terms/pallas_call | solution.py:192
  98.8 2.0 %collective-permute-done.9 = bf16[4,4,2,128,128]{4,3,2,1,0:T(8,128)(2,1)S(1)} collective-permute-done((bf16[4,4,2,128,128]{4,3,2,1,0:T(8,128)(2,1)}, bf16[4,4,2,128,128]{4,3,2,1,0:T(8,128)(2,1)S(1)}, u32[]{:S(2)}, u32[]{:S(2)}) %collective-permute-start.9) | collective-permute-done | bytes 1048608 | tf_op jit(solution)/shard_map/ppermute | solution.py:221
  100.8 1.6 %add_convert_fusion = bf16[4,4,2,128,128]{4,3,2,1,0:T(8,128)(2,1)S(1)} fusion(bf16[4,4,2,128,128]{4,3,2,1,0:T(8,128)(2,1)S(1)} %collective-permute-done.9, bf16[4,4,2,128,128]{4,3,2,1,0:T(8,128)(2,1)} %terms.2), kind=kLoop, calls=%fused_computation | loop fusion | flops 2097152 | bytes 3145728 | tf_op jit(solution)/shard_map/convert_element_type | solution.py:223
  102.4 36.9 %all_to_all.10 = bf16[16,2,128,128]{3,2,1,0:T(8,128)(2,1)S(1)} all-to-all(bf16[16,2,128,128]{3,2,1,0:T(8,128)(2,1)S(1)} %bitcast.22), channel_id=1, replica_groups=mesh['z'=8,'x'=4,'c'=2,'yh'=4,'yl'=2] {'x','yh'}, dimensions={0} | all-to-all | bytes 2097152 | tf_op jit(solution)/shard_map/all_to_all | solution.py:225
  139.3 0.9 bitcast_reduce_fusion
Async XLA Ops:
  0.0 28.0 %copy-start.7 = (bf16[8,64,128]{2,1,0:T(8,128)(2,1)S(1)}, bf16[8,64,128]{2,1,0:T(8,128)(2,1)}, u32[]{:S(2)}) copy-start(bf16[8,64,128]{2,1,0:T(8,128)(2,1)} %param.7) | copy-start | bytes 393220
  4.5 33.7 %collective-permute-start.1 = (bf16[528,1152]{1,0:T(8,128)(2,1)}, bf16[528,1152]{1,0:T(8,128)(2,1)S(1)}, u32[]{:S(2)}, u32[]{:S(2)}) collective-permute-start(bf16[528,1152]{1,0:T(8,128)(2,1)} %get-tuple-element.7.refs_0_), channel_id=1, source_target_pairs={{0,48},{16,0},{32,16},{48,32},{1,49},{17,1},{33,17},{49,33},{2,50}... | collective-permute-start | bytes 3649544 | tf_op jit(solution)/shard_map/ppermute | solution.py:155
  9.7 28.5 %collective-permute-start = (bf16[528,1152]{1,0:T(8,128)(2,1)}, bf16[528,1152]{1,0:T(8,128)(2,1)S(1)}, u32[]{:S(2)}, u32[]{:S(2)}) collective-permute-start(bf16[528,1152]{1,0:T(8,128)(2,1)} %get-tuple-element.7.refs_0_), channel_id=1, source_target_pairs={{0,16},{16,32},{32,48},{48,0},{1,17},{17,33},{33,49},{49,1},{2,18}... | collective-permute-start | bytes 3649544 | tf_op jit(solution)/shard_map/ppermute | solution.py:155
  11.6 8.7 %collective-permute-start.3 = (bf16[528,128]{1,0:T(8,128)(2,1)}, bf16[528,128]{1,0:T(8,128)(2,1)S(1)}, u32[]{:S(2)}, u32[]{:S(2)}) collective-permute-start(bf16[528,128]{1,0:T(8,128)(2,1)} %get-tuple-element.8), channel_id=1, source_target_pairs={{0,8},{8,0},{1,9},{9,1},{2,10},{10,2},{3,11},{11,3},{4,12},{12,4},... | collective-permute-start | bytes 405512 | tf_op jit(solution)/shard_map/ppermute | solution.py:155
  22.0 14.0 %collective-permute-start.4 = (bf16[2,528,128]{2,1,0:T(8,128)(2,1)}, bf16[2,528,128]{2,1,0:T(8,128)(2,1)}, u32[]{:S(2)}, u32[]{:S(2)}) collective-permute-start(bf16[2,528,128]{2,1,0:T(8,128)(2,1)} %pad_maximum_fusion.1.refs_4_), channel_id=1, source_target_pairs={{0,64},{8,456},{64,128},{72,8},{128,192},{136,72},{192,256},{200,1... | collective-permute-start | bytes 811016 | tf_op jit(solution)/shard_map/ppermute | solution.py:180
  29.1 42.5 %all-to-all-start = ((bf16[8,512,128]{2,1,0:T(8,128)(2,1)}), bf16[8,512,128]{2,1,0:T(8,128)(2,1)S(1)}, u32[]{:S(2)}, u32[]{:S(2)}) async-start(bf16[8,512,128]{2,1,0:T(8,128)(2,1)} %broadcast_in_dim.2), calls=%async_computation | async-start | bytes 2097152 | tf_op jit(solution)/shard_map/all_to_all | solution.py:173
  36.0 9.0 %collective-permute-start.5 = (bf16[2,528,128]{2,1,0:T(8,128)(2,1)}, bf16[2,528,128]{2,1,0:T(8,128)(2,1)S(1)}, u32[]{:S(2)}, u32[]{:S(2)}) collective-permute-start(bf16[2,528,128]{2,1,0:T(8,128)(2,1)} %collective-permute-done.4.refs_5_), channel_id=1, source_target_pairs={{0,64},{8,456},{64,128},{72,8},{128,192},{136,72},{192,256},{200,1... | collective-permute-start | bytes 811016 | tf_op jit(solution)/shard_map/ppermute | solution.py:181
  38.2 1.5 %copy-start = (bf16[528,1152]{1,0:T(8,128)(2,1)}, bf16[528,1152]{1,0:T(8,128)(2,1)S(1)}, u32[]{:S(2)}) copy-start(bf16[528,1152]{1,0:T(8,128)(2,1)S(1)} %collective-permute-done.1.refs_3_) | copy-start | bytes 3649540
  38.2 1.8 %copy-start.1 = (bf16[528,1152]{1,0:T(8,128)(2,1)}, bf16[528,1152]{1,0:T(8,128)(2,1)S(1)}, u32[]{:S(2)}) copy-start(bf16[528,1152]{1,0:T(8,128)(2,1)S(1)} %collective-permute-done.refs_1_) | copy-start | bytes 3649540
  40.0 27.9 %copy-start.8 = (s32[1,8,8]{2,1,0:T(8,128)S(1)}, s32[1,8,8]{2,1,0:T(8,128)}, u32[]{:S(2)}) copy-start(s32[1,8,8]{2,1,0:T(8,128)} %param.10) | copy-start | bytes 772
  40.0 31.7 %collective-permute-start.2 = (bf16[528,1152]{1,0:T(8,128)(2,1)}, bf16[528,1152]{1,0:T(8,128)(2,1)}, u32[]{:S(2)}, u32[]{:S(2)}) collective-permute-start(bf16[528,1152]{1,0:T(8,128)(2,1)} %broadcast_select_fusion), channel_id=1, source_target_pairs={{0,16},{8,56},{16,32},{24,8},{32,48},{40,24},{48,0},{56,40},{1,17}... | collective-permute-start | bytes 3649544 | tf_op jit(solution)/shard_map/ppermute | solution.py:185
  45.0 12.9 %copy-start.4 = (bf16[2,528,128]{2,1,0:T(8,128)(2,1)}, bf16[2,528,128]{2,1,0:T(8,128)(2,1)S(1)}, u32[]{:S(2)}) copy-start(bf16[2,528,128]{2,1,0:T(8,128)(2,1)S(1)} %collective-permute-done.5.refs_6_) | copy-start | bytes 811012
  45.0 12.9 %collective-permute-start.6 = (bf16[2,528,128]{2,1,0:T(8,128)(2,1)S(1)}, bf16[2,528,128]{2,1,0:T(8,128)(2,1)S(1)}, u32[]{:S(2)}, u32[]{:S(2)}) collective-permute-start(bf16[2,528,128]{2,1,0:T(8,128)(2,1)S(1)} %collective-permute-done.5.refs_6_), channel_id=1, source_target_pairs={{0,64},{8,456},{64,128},{72,8},{128,192},{136,72},{192,256},{200,1... | collective-permute-start | bytes 811016 | tf_op jit(solution)/shard_map/ppermute | solution.py:182
  57.9 13.8 %copy-start.5 = (bf16[2,528,128]{2,1,0:T(8,128)(2,1)}, bf16[2,528,128]{2,1,0:T(8,128)(2,1)S(1)}, u32[]{:S(2)}) copy-start(bf16[2,528,128]{2,1,0:T(8,128)(2,1)S(1)} %collective-permute-done.6.refs_7_) | copy-start | bytes 811012
  59.0 12.6 %collective-permute-start.8 = (bf16[3,2,528,128]{3,2,1,0:T(8,128)(2,1)S(1)}, bf16[3,2,528,128]{3,2,1,0:T(8,128)(2,1)S(1)}, u32[]{:S(2)}, u32[]{:S(2)}) collective-permute-start(bf16[3,2,528,128]{3,2,1,0:T(8,128)(2,1)S(1)} %pad_maximum_fusion), channel_id=1, source_target_pairs={{0,8},{8,0},{1,9},{9,1},{2,10},{10,2},{3,11},{11,3},{4,12},{12,4},... | collective-permute-start | bytes 2433032 | tf_op jit(solution)/shard_map/ppermute | solution.py:155
  64.1 7.5 %collective-permute-start.7 = (bf16[2,528,128]{2,1,0:T(8,128)(2,1)S(1)}, bf16[2,528,128]{2,1,0:T(8,128)(2,1)S(1)}, u32[]{:S(2)}, u32[]{:S(2)}) collective-permute-start(bf16[2,528,128]{2,1,0:T(8,128)(2,1)S(1)} %collective-permute-done.6.refs_7_), channel_id=1, source_target_pairs={{0,64},{8,456},{64,128},{72,8},{128,192},{136,72},{192,256},{200,1... | collective-permute-start | bytes 811016 | tf_op jit(solution)/shard_map/ppermute | solution.py:183
  71.6 0.7 copy-start.6
  71.6 1.0 copy-start.3
  71.7 1.3 copy-start.2
  82.8 18.0 %collective-permute-start.9 = (bf16[4,4,2,128,128]{4,3,2,1,0:T(8,128)(2,1)}, bf16[4,4,2,128,128]{4,3,2,1,0:T(8,128)(2,1)S(1)}, u32[]{:S(2)}, u32[]{:S(2)}) collective-permute-start(bf16[4,4,2,128,128]{4,3,2,1,0:T(8,128)(2,1)} %terms.3), channel_id=1, source_target_pairs={{0,1},{1,0},{2,3},{3,2},{4,5},{5,4},{6,7},{7,6},{8,15},{9,10},{10,... | collective-permute-start | bytes 3145736 | tf_op jit(solution)/shard_map/ppermute | solution.py:221

commit v5 on v4

--- a/solution.py
+++ b/solution.py
@@ -51,7 +51,7 @@
     tables = [pltpu.make_async_copy(*spot, sems.at[NX + at]) for at, spot in enumerate(spots)]
     after = NX + len(tables)
     near_copy = pltpu.make_async_copy(near_hbm, near_ref, sems.at[after])
-    for copy in copies[:1] + tables + [near_copy] + copies[1:]:
+    for copy in copies[:1] + [near_copy] + copies[1:] + tables:
         copy.start()
     slots = lax.broadcasted_iota(I32, (RB, CW), 0) * SA + lax.broadcasted_iota(I32, (RB, CW), 1)
     moves = [
@@ -64,6 +64,52 @@
     items_v[NX, :, :SA] = jnp.where(close, slots[:, :SA] | (entry << 7) | (1 << FLAG), 0)
     moves[NX].start()
     acc[...] = jnp.zeros_like(acc)
+    near_start = NX * SLOTS + UNROLL
+
+    def select(first, turns, start):
+        def pick(at, count):
+            for s in range(SA):
+                item = items[first + (at >> 3), at & 7, s]
+                todo[start + count] = item
+                count = count + (item >> FLAG)
+            return count
+
+        count = lax.fori_loop(0, turns * RB, pick, 0)
+        for u in range(UNROLL):
+            todo[start + count + u] = 0
+        return count
+
+    def add_terms(start, count, turns, block_of, panel_of):
+        def body(step, unused):
+            found = []
+            for u in range(UNROLL):
+                item = todo[start + step * UNROLL + u]
+                slot = item & (SLOTS * turns - 1)
+                block = block_of(item)
+                odd = (slot & 1) == 1
+                zero = jnp.zeros_like(block)
+                right = jnp.concatenate([jnp.where(odd, zero, block), jnp.where(odd, block, zero)], 0)
+                term = jnp.dot(left[slot >> 1], right, preferred_element_type=F32)
+                found.append((jnp.where((item >> FLAG) == 1, panel_of(item), NX * NZ), term))
+            for panel, term in found:
+                acc[panel] += term
+            return 0
+
+        lax.fori_loop(0, (count + UNROLL - 1) // UNROLL, body, 0)
+
+    def near_block(item):
+        entry = (item >> 7) & 127
+        listed = jnp.maximum(entry - RB, 0)
+        member = jnp.where(entry < RB, my_y, listed >> 3)
+        row = jnp.where(entry < RB, entry, need[listed])
+        return near_ref[member, pl.ds(pl.multiple_of(row * BS, BS), BS), :]
+
+    def far_block(item):
+        panel = (item >> 12) & 15
+        group = (my_x - ((item >> 7) & 3)) & (NX - 1)
+        other = (panel & 1) ^ my_c
+        row = (sent[panel >> 1, (item >> 9) & 7, (my_z * NX + group) * NC + my_c] >> (other * 3)) & 7
+        return p_ref[panel >> 1, other, pl.ds(pl.multiple_of(row * BS, BS), BS), :]
 
     for turn in range(NX):
         copies[turn].wait()
@@ -82,64 +128,19 @@
             ).astype(BF16)
             for pair in range(SA // 2):
                 left[(turn * RB + n) * (SA // 2) + pair] = product[:, pair * CW : (pair + 1) * CW]
+        if turn == 0:
+            moves[NX].wait()
+            near_count = select(NX, 1, near_start)
+            near_copy.wait()
+            add_terms(near_start, near_count, 1, near_block, lambda item: (my_z >> 1) * NC + my_c)
     for copy in tables:
         copy.wait()
     both = p_ref[:, :, pl.ds(PROWS, PAD), :].astype(F32)[:, :, :RB].astype(I32)
     sent_v[...] = both[:, 0] | (both[:, 1] << 3)
     list_move.start()
-
-    def select(first, turns, start):
-        def pick(at, count):
-            for s in range(SA):
-                item = items[first + (at >> 3), at & 7, s]
-                todo[start + count] = item
-                count = count + (item >> FLAG)
-            return count
-
-        count = lax.fori_loop(0, turns * RB, pick, 0)
-        for u in range(UNROLL):
-            todo[start + count + u] = 0
-        return count
-
-    def add_terms(start, count, turns, block_of, panel_of):
-        def body(step, unused):
-            found = []
-            for u in range(UNROLL):
-                item = todo[start + step * UNROLL + u]
-                slot = item & (SLOTS * turns - 1)
-                block = block_of(item)
-                odd = (slot & 1) == 1
-                zero = jnp.zeros_like(block)
-                right = jnp.concatenate([jnp.where(odd, zero, block), jnp.where(odd, block, zero)], 0)
-                term = jnp.dot(left[slot >> 1], right, preferred_element_type=F32)
-                found.append((jnp.where((item >> FLAG) == 1, panel_of(item), NX * NZ), term))
-            for panel, term in found:
-                acc[panel] += term
-            return 0
-
-        lax.fori_loop(0, (count + UNROLL - 1) // UNROLL, body, 0)
-
-    def near_block(item):
-        entry = (item >> 7) & 127
-        listed = jnp.maximum(entry - RB, 0)
-        member = jnp.where(entry < RB, my_y, listed >> 3)
-        row = jnp.where(entry < RB, entry, need[listed])
-        return near_ref[member, pl.ds(pl.multiple_of(row * BS, BS), BS), :]
-
-    def far_block(item):
-        panel = (item >> 12) & 15
-        group = (my_x - ((item >> 7) & 3)) & (NX - 1)
-        other = (panel & 1) ^ my_c
-        row = (sent[panel >> 1, (item >> 9) & 7, (my_z * NX + group) * NC + my_c] >> (other * 3)) & 7
-        return p_ref[panel >> 1, other, pl.ds(pl.multiple_of(row * BS, BS), BS), :]
-
-    for move in moves:
+    for move in moves[:NX]:
         move.wait()
-    near_start = NX * SLOTS + UNROLL
-    near_count = select(NX, 1, near_start)
     far_count = select(0, NX, 0)
-    near_copy.wait()
-    add_terms(near_start, near_count, 1, near_block, lambda item: (my_z >> 1) * NC + my_c)
     list_move.wait()
     add_terms(
         0, far_count, NX, far_block,

time: 141 us -> 140 us (level)
  no operation moved by 1% of the time
where the time goes in v5:
time: 140 us; the launch traced here: 139 us
  starting transfers between devices  58 us (41%)
  blocking collectives  36.7 us (26%)
  Pallas kernels  22.2 us (16%)
  waiting for transfers between devices  9.05 us (6%)
  other arithmetic  6.57 us (5%)
  local copies, waits for them, and re-layouts  5.96 us (4%)
    all_to_all x1, blocking collectives, shards(): lax.all_to_all(partial.reshape(NX * NY // 2, NC, CW, CW), ('x', 'yh'), sp...  36.7 us
    ppermute x4, starting transfers between devices, hop(): lax.ppermute(array, axis, [(i, (i + step) % size) for i in range(size)])  19.7 us
    pallas_call x2, Pallas kernels, terms(): pl.pallas_call(terms_kernel, out_shape=jax.ShapeDtypeStruct((NX, NZ // 2,...  19.6 us
    ppermute x1, starting transfers between devices, shards(): three = lax.ppermute(two, ('z', 'c'), around)  9.54 us
    all_to_all x1, starting transfers between devices, shards(): lax.all_to_all(jnp.broadcast_to(own_p[None], (NY, PROWS, CW)), ('yh', 'yl...  6.82 us
    ppermute x1, starting transfers between devices, shards(): one = lax.ppermute(here, ('z', 'c'), around)  6.03 us
    ppermute x1, starting transfers between devices, shards(): given = lax.ppermute(terms(1 - (my_y & 1)), ('c', 'yh', 'yl'), pairs)  5.04 us
    ppermute x1, starting transfers between devices, shards(): lax.ppermute(jnp.where(my_c == 0, low, high), ('x', 'c'), [(x * NC + c, (...  4.97 us
  transfers between devices with their start and end apart: 11, of which 4 were waited for; matrix products, arithmetic and copies ran while one was open for 5% of the time, Pallas kernels for 7%

profile of v5, /device:TPU:1, one launch (start us, length us, event | category | flops | bytes accessed | tf_op | source)
XLA Modules:
  0.0 139.3 jit_solution(364499143318565576)
XLA Ops:
  0.0 0.0 copy-start.7
  0.7 1.3 copy.9
  2.0 2.5 %pack.1 = (bf16[528,1152]{1,0:T(8,128)(2,1)}, bf16[528,128]{1,0:T(8,128)(2,1)}) custom-call(s32[1]{0:T(128)S(6)} %copy.10.live, bf16[512,1024]{1,0:T(8,128)(2,1)} %bitcast.25, bf16[512,128]{1,0:T(8,128)(2,1)} %bitcast.26, s32[8,16]{1,0:T(8,128)} %cols.5, s32[6,64]{1,0:T(8,128)} %bitcast.30), custom_call_target="tpu_custom_call" | custom-call | tf_op jit(solution)/shard_map/pack/pallas_call | solution.py:164
  4.5 5.2 %collective-permute-start.1 = (bf16[528,1152]{1,0:T(8,128)(2,1)}, bf16[528,1152]{1,0:T(8,128)(2,1)S(1)}, u32[]{:S(2)}, u32[]{:S(2)}) collective-permute-start(bf16[528,1152]{1,0:T(8,128)(2,1)} %get-tuple-element.7.refs_0_), channel_id=1, source_target_pairs={{0,48},{16,0},{32,16},{48,32},{1,49},{17,1},{33,17},{49,33},{2,50}... | collective-permute-start | bytes 3649544 | tf_op jit(solution)/shard_map/ppermute | solution.py:156
  9.7 1.9 %collective-permute-start = (bf16[528,1152]{1,0:T(8,128)(2,1)}, bf16[528,1152]{1,0:T(8,128)(2,1)S(1)}, u32[]{:S(2)}, u32[]{:S(2)}) collective-permute-start(bf16[528,1152]{1,0:T(8,128)(2,1)} %get-tuple-element.7.refs_0_), channel_id=1, source_target_pairs={{0,16},{16,32},{32,48},{48,0},{1,17},{17,33},{33,49},{49,1},{2,18}... | collective-permute-start | bytes 3649544 | tf_op jit(solution)/shard_map/ppermute | solution.py:156
  11.6 7.5 %collective-permute-start.3 = (bf16[528,128]{1,0:T(8,128)(2,1)}, bf16[528,128]{1,0:T(8,128)(2,1)S(1)}, u32[]{:S(2)}, u32[]{:S(2)}) collective-permute-start(bf16[528,128]{1,0:T(8,128)(2,1)} %get-tuple-element.8), channel_id=1, source_target_pairs={{0,8},{8,0},{1,9},{9,1},{2,10},{10,2},{3,11},{11,3},{4,12},{12,4},... | collective-permute-start | bytes 405512 | tf_op jit(solution)/shard_map/ppermute | solution.py:156
  19.1 1.2 collective-permute-done.3
  20.3 1.7 %pad_maximum_fusion.1.refs_4_ = bf16[2,528,128]{2,1,0:T(8,128)(2,1)} fusion(bf16[1,528,128]{2,1,0:T(8,128)(2,1)S(1)} %bitcast.29, bf16[1,528,128]{2,1,0:T(8,128)(2,1)} %bitcast.28), kind=kLoop, calls=%fused_computation.4 | loop fusion | flops 135168 | bytes 540672 | tf_op jit(solution)/shard_map/stack | solution.py:180
  22.0 6.0 %collective-permute-start.4 = (bf16[2,528,128]{2,1,0:T(8,128)(2,1)}, bf16[2,528,128]{2,1,0:T(8,128)(2,1)}, u32[]{:S(2)}, u32[]{:S(2)}) collective-permute-start(bf16[2,528,128]{2,1,0:T(8,128)(2,1)} %pad_maximum_fusion.1.refs_4_), channel_id=1, source_target_pairs={{0,64},{8,456},{64,128},{72,8},{128,192},{136,72},{192,256},{200,1... | collective-permute-start | bytes 811016 | tf_op jit(solution)/shard_map/ppermute | solution.py:181
  28.0 0.0 copy-done.7
  28.0 1.1 broadcast_in_dim.2
  29.1 6.8 %all-to-all-start = ((bf16[8,512,128]{2,1,0:T(8,128)(2,1)}), bf16[8,512,128]{2,1,0:T(8,128)(2,1)S(1)}, u32[]{:S(2)}, u32[]{:S(2)}) async-start(bf16[8,512,128]{2,1,0:T(8,128)(2,1)} %broadcast_in_dim.2), calls=%async_computation | async-start | bytes 2097152 | tf_op jit(solution)/shard_map/all_to_all | solution.py:174
  36.0 0.0 collective-permute-done.4.refs_5_
  36.0 2.2 %collective-permute-start.5 = (bf16[2,528,128]{2,1,0:T(8,128)(2,1)}, bf16[2,528,128]{2,1,0:T(8,128)(2,1)S(1)}, u32[]{:S(2)}, u32[]{:S(2)}) collective-permute-start(bf16[2,528,128]{2,1,0:T(8,128)(2,1)} %collective-permute-done.4.refs_5_), channel_id=1, source_target_pairs={{0,64},{8,456},{64,128},{72,8},{128,192},{136,72},{192,256},{200,1... | collective-permute-start | bytes 811016 | tf_op jit(solution)/shard_map/ppermute | solution.py:182
  38.2 0.0 collective-permute-done.1.refs_3_
  38.2 0.0 copy-start
  38.2 0.0 collective-permute-done.refs_1_
  38.2 0.0 copy-start.1
  38.2 1.3 broadcast_select_fusion
  39.5 0.1 copy-done
  39.7 0.3 copy-done.1
  40.0 0.0 copy-start.8
  40.0 5.0 %collective-permute-start.2 = (bf16[528,1152]{1,0:T(8,128)(2,1)}, bf16[528,1152]{1,0:T(8,128)(2,1)}, u32[]{:S(2)}, u32[]{:S(2)}) collective-permute-start(bf16[528,1152]{1,0:T(8,128)(2,1)} %broadcast_select_fusion), channel_id=1, source_target_pairs={{0,16},{8,56},{16,32},{24,8},{32,48},{40,24},{48,0},{56,40},{1,17}... | collective-permute-start | bytes 3649544 | tf_op jit(solution)/shard_map/ppermute | solution.py:186
  44.9 0.0 collective-permute-done.5.refs_6_
  45.0 0.0 copy-start.4
  45.0 9.5 %collective-permute-start.6 = (bf16[2,528,128]{2,1,0:T(8,128)(2,1)S(1)}, bf16[2,528,128]{2,1,0:T(8,128)(2,1)S(1)}, u32[]{:S(2)}, u32[]{:S(2)}) collective-permute-start(bf16[2,528,128]{2,1,0:T(8,128)(2,1)S(1)} %collective-permute-done.5.refs_6_), channel_id=1, source_target_pairs={{0,64},{8,456},{64,128},{72,8},{128,192},{136,72},{192,256},{200,1... | collective-permute-start | bytes 811016 | tf_op jit(solution)/shard_map/ppermute | solution.py:183
  54.5 3.4 %collective-permute-done.6.refs_7_ = bf16[2,528,128]{2,1,0:T(8,128)(2,1)S(1)} collective-permute-done((bf16[2,528,128]{2,1,0:T(8,128)(2,1)S(1)}, bf16[2,528,128]{2,1,0:T(8,128)(2,1)S(1)}, u32[]{:S(2)}, u32[]{:S(2)}) %collective-permute-start.6) | collective-permute-done | bytes 270368 | tf_op jit(solution)/shard_map/ppermute | solution.py:183
  57.9 0.0 copy-start.5
  57.9 0.0 copy-done.4
  57.9 1.1 pad_maximum_fusion
  59.0 5.1 %collective-permute-start.8 = (bf16[3,2,528,128]{3,2,1,0:T(8,128)(2,1)S(1)}, bf16[3,2,528,128]{3,2,1,0:T(8,128)(2,1)S(1)}, u32[]{:S(2)}, u32[]{:S(2)}) collective-permute-start(bf16[3,2,528,128]{3,2,1,0:T(8,128)(2,1)S(1)} %pad_maximum_fusion), channel_id=1, source_target_pairs={{0,8},{8,0},{1,9},{9,1},{2,10},{10,2},{3,11},{11,3},{4,12},{12,4},... | collective-permute-start | bytes 2433032 | tf_op jit(solution)/shard_map/ppermute | solution.py:156
  64.1 3.6 %collective-permute-start.7 = (bf16[2,528,128]{2,1,0:T(8,128)(2,1)S(1)}, bf16[2,528,128]{2,1,0:T(8,128)(2,1)S(1)}, u32[]{:S(2)}, u32[]{:S(2)}) collective-permute-start(bf16[2,528,128]{2,1,0:T(8,128)(2,1)S(1)} %collective-permute-done.6.refs_7_), channel_id=1, source_target_pairs={{0,64},{8,456},{64,128},{72,8},{128,192},{136,72},{192,256},{200,1... | collective-permute-start | bytes 811016 | tf_op jit(solution)/shard_map/ppermute | solution.py:184
  67.8 0.0 copy-done.8
  67.8 0.6 reshape.20.need
  68.4 0.6 stack.63.place
  69.0 2.6 %collective-permute-done.7.refs_8_ = bf16[2,528,128]{2,1,0:T(8,128)(2,1)S(1)} collective-permute-done((bf16[2,528,128]{2,1,0:T(8,128)(2,1)S(1)}, bf16[2,528,128]{2,1,0:T(8,128)(2,1)S(1)}, u32[]{:S(2)}, u32[]{:S(2)}) %collective-permute-start.7) | collective-permute-done | bytes 270368 | tf_op jit(solution)/shard_map/ppermute | solution.py:184
  71.6 0.0 copy-start.6
  71.6 0.0 collective-permute-done.8.refs_9_
  71.6 0.0 copy-start.3
  71.7 0.0 all-to-all-done.refs_10_
  71.7 0.0 copy-start.2
  71.7 0.0 collective-permute-done.2.refs_2_
  71.7 0.0 copy-done.5
  71.7 0.7 copy-done.6
  72.4 0.3 copy-done.3
  72.7 0.3 copy-done.2
  73.0 9.7 %terms.3 = bf16[4,4,2,128,128]{4,3,2,1,0:T(8,128)(2,1)} custom-call(s32[6]{0:T(128)} %stack.63.place, s32[64]{0:T(128)} %reshape.20.need, s32[8,16]{1,0:T(8,128)} %cols.5, bf16[528,1152]{1,0:T(8,128)(2,1)} %get-tuple-element.7.refs_0_, bf16[528,1152]{1,0:T(8,128)(2,1)} %copy-done.1, bf16[528,1152]{1,0:T(8,128)(2,1)} %collective-permute-done.2.refs_2_, ...), custom_call_target="tpu_custom_call" | custom-call | flops 2000000000 | bytes 12000000 | tf_op jit(solution)/shard_map/terms/pallas_call | solution.py:193
  82.7 5.0 %collective-permute-start.9 = (bf16[4,4,2,128,128]{4,3,2,1,0:T(8,128)(2,1)}, bf16[4,4,2,128,128]{4,3,2,1,0:T(8,128)(2,1)S(1)}, u32[]{:S(2)}, u32[]{:S(2)}) collective-permute-start(bf16[4,4,2,128,128]{4,3,2,1,0:T(8,128)(2,1)} %terms.3), channel_id=1, source_target_pairs={{0,1},{1,0},{2,3},{3,2},{4,5},{5,4},{6,7},{7,6},{8,15},{9,10},{10,... | collective-permute-start | bytes 3145736 | tf_op jit(solution)/shard_map/ppermute | solution.py:222
  87.8 0.6 stack.54.place
  88.4 9.9 %terms.2 = bf16[4,4,2,128,128]{4,3,2,1,0:T(8,128)(2,1)} custom-call(s32[6]{0:T(128)} %stack.54.place, s32[64]{0:T(128)} %reshape.20.need, s32[8,16]{1,0:T(8,128)} %cols.5, bf16[528,1152]{1,0:T(8,128)(2,1)} %get-tuple-element.7.refs_0_, bf16[528,1152]{1,0:T(8,128)(2,1)} %copy-done.1, bf16[528,1152]{1,0:T(8,128)(2,1)} %collective-permute-done.2.refs_2_, ...), custom_call_target="tpu_custom_call" | custom-call | flops 2000000000 | bytes 12000000 | tf_op jit(solution)/shard_map/terms/pallas_call | solution.py:193
  98.3 1.8 %collective-permute-done.9 = bf16[4,4,2,128,128]{4,3,2,1,0:T(8,128)(2,1)S(1)} collective-permute-done((bf16[4,4,2,128,128]{4,3,2,1,0:T(8,128)(2,1)}, bf16[4,4,2,128,128]{4,3,2,1,0:T(8,128)(2,1)S(1)}, u32[]{:S(2)}, u32[]{:S(2)}) %collective-permute-start.9) | collective-permute-done | bytes 1048608 | tf_op jit(solution)/shard_map/ppermute | solution.py:222
  100.2 1.6 %add_convert_fusion = bf16[4,4,2,128,128]{4,3,2,1,0:T(8,128)(2,1)S(1)} fusion(bf16[4,4,2,128,128]{4,3,2,1,0:T(8,128)(2,1)S(1)} %collective-permute-done.9, bf16[4,4,2,128,128]{4,3,2,1,0:T(8,128)(2,1)} %terms.2), kind=kLoop, calls=%fused_computation | loop fusion | flops 2097152 | bytes 3145728 | tf_op jit(solution)/shard_map/convert_element_type | solution.py:224
  101.8 36.7 %all_to_all.10 = bf16[16,2,128,128]{3,2,1,0:T(8,128)(2,1)S(1)} all-to-all(bf16[16,2,128,128]{3,2,1,0:T(8,128)(2,1)S(1)} %bitcast.22), channel_id=1, replica_groups=mesh['z'=8,'x'=4,'c'=2,'yh'=4,'yl'=2] {'x','yh'}, dimensions={0} | all-to-all | bytes 2097152 | tf_op jit(solution)/shard_map/all_to_all | solution.py:226
  138.4 0.9 bitcast_reduce_fusion
Async XLA Ops:
  0.0 28.0 %copy-start.7 = (bf16[8,64,128]{2,1,0:T(8,128)(2,1)S(1)}, bf16[8,64,128]{2,1,0:T(8,128)(2,1)}, u32[]{:S(2)}) copy-start(bf16[8,64,128]{2,1,0:T(8,128)(2,1)} %param.7) | copy-start | bytes 393220
  4.5 33.7 %collective-permute-start.1 = (bf16[528,1152]{1,0:T(8,128)(2,1)}, bf16[528,1152]{1,0:T(8,128)(2,1)S(1)}, u32[]{:S(2)}, u32[]{:S(2)}) collective-permute-start(bf16[528,1152]{1,0:T(8,128)(2,1)} %get-tuple-element.7.refs_0_), channel_id=1, source_target_pairs={{0,48},{16,0},{32,16},{48,32},{1,49},{17,1},{33,17},{49,33},{2,50}... | collective-permute-start | bytes 3649544 | tf_op jit(solution)/shard_map/ppermute | solution.py:156
  9.7 28.5 %collective-permute-start = (bf16[528,1152]{1,0:T(8,128)(2,1)}, bf16[528,1152]{1,0:T(8,128)(2,1)S(1)}, u32[]{:S(2)}, u32[]{:S(2)}) collective-permute-start(bf16[528,1152]{1,0:T(8,128)(2,1)} %get-tuple-element.7.refs_0_), channel_id=1, source_target_pairs={{0,16},{16,32},{32,48},{48,0},{1,17},{17,33},{33,49},{49,1},{2,18}... | collective-permute-start | bytes 3649544 | tf_op jit(solution)/shard_map/ppermute | solution.py:156
  11.6 8.7 %collective-permute-start.3 = (bf16[528,128]{1,0:T(8,128)(2,1)}, bf16[528,128]{1,0:T(8,128)(2,1)S(1)}, u32[]{:S(2)}, u32[]{:S(2)}) collective-permute-start(bf16[528,128]{1,0:T(8,128)(2,1)} %get-tuple-element.8), channel_id=1, source_target_pairs={{0,8},{8,0},{1,9},{9,1},{2,10},{10,2},{3,11},{11,3},{4,12},{12,4},... | collective-permute-start | bytes 405512 | tf_op jit(solution)/shard_map/ppermute | solution.py:156
  22.0 14.0 %collective-permute-start.4 = (bf16[2,528,128]{2,1,0:T(8,128)(2,1)}, bf16[2,528,128]{2,1,0:T(8,128)(2,1)}, u32[]{:S(2)}, u32[]{:S(2)}) collective-permute-start(bf16[2,528,128]{2,1,0:T(8,128)(2,1)} %pad_maximum_fusion.1.refs_4_), channel_id=1, source_target_pairs={{0,64},{8,456},{64,128},{72,8},{128,192},{136,72},{192,256},{200,1... | collective-permute-start | bytes 811016 | tf_op jit(solution)/shard_map/ppermute | solution.py:181
  29.1 42.5 %all-to-all-start = ((bf16[8,512,128]{2,1,0:T(8,128)(2,1)}), bf16[8,512,128]{2,1,0:T(8,128)(2,1)S(1)}, u32[]{:S(2)}, u32[]{:S(2)}) async-start(bf16[8,512,128]{2,1,0:T(8,128)(2,1)} %broadcast_in_dim.2), calls=%async_computation | async-start | bytes 2097152 | tf_op jit(solution)/shard_map/all_to_all | solution.py:174
  36.0 9.0 %collective-permute-start.5 = (bf16[2,528,128]{2,1,0:T(8,128)(2,1)}, bf16[2,528,128]{2,1,0:T(8,128)(2,1)S(1)}, u32[]{:S(2)}, u32[]{:S(2)}) collective-permute-start(bf16[2,528,128]{2,1,0:T(8,128)(2,1)} %collective-permute-done.4.refs_5_), channel_id=1, source_target_pairs={{0,64},{8,456},{64,128},{72,8},{128,192},{136,72},{192,256},{200,1... | collective-permute-start | bytes 811016 | tf_op jit(solution)/shard_map/ppermute | solution.py:182
  38.2 1.5 %copy-start = (bf16[528,1152]{1,0:T(8,128)(2,1)}, bf16[528,1152]{1,0:T(8,128)(2,1)S(1)}, u32[]{:S(2)}) copy-start(bf16[528,1152]{1,0:T(8,128)(2,1)S(1)} %collective-permute-done.1.refs_3_) | copy-start | bytes 3649540
  38.2 1.8 %copy-start.1 = (bf16[528,1152]{1,0:T(8,128)(2,1)}, bf16[528,1152]{1,0:T(8,128)(2,1)S(1)}, u32[]{:S(2)}) copy-start(bf16[528,1152]{1,0:T(8,128)(2,1)S(1)} %collective-permute-done.refs_1_) | copy-start | bytes 3649540
  40.0 27.9 %copy-start.8 = (s32[1,8,8]{2,1,0:T(8,128)S(1)}, s32[1,8,8]{2,1,0:T(8,128)}, u32[]{:S(2)}) copy-start(s32[1,8,8]{2,1,0:T(8,128)} %param.10) | copy-start | bytes 772
  40.0 31.7 %collective-permute-start.2 = (bf16[528,1152]{1,0:T(8,128)(2,1)}, bf16[528,1152]{1,0:T(8,128)(2,1)}, u32[]{:S(2)}, u32[]{:S(2)}) collective-permute-start(bf16[528,1152]{1,0:T(8,128)(2,1)} %broadcast_select_fusion), channel_id=1, source_target_pairs={{0,16},{8,56},{16,32},{24,8},{32,48},{40,24},{48,0},{56,40},{1,17}... | collective-permute-start | bytes 3649544 | tf_op jit(solution)/shard_map/ppermute | solution.py:186
  45.0 12.9 %copy-start.4 = (bf16[2,528,128]{2,1,0:T(8,128)(2,1)}, bf16[2,528,128]{2,1,0:T(8,128)(2,1)S(1)}, u32[]{:S(2)}) copy-start(bf16[2,528,128]{2,1,0:T(8,128)(2,1)S(1)} %collective-permute-done.5.refs_6_) | copy-start | bytes 811012
  45.0 12.9 %collective-permute-start.6 = (bf16[2,528,128]{2,1,0:T(8,128)(2,1)S(1)}, bf16[2,528,128]{2,1,0:T(8,128)(2,1)S(1)}, u32[]{:S(2)}, u32[]{:S(2)}) collective-permute-start(bf16[2,528,128]{2,1,0:T(8,128)(2,1)S(1)} %collective-permute-done.5.refs_6_), channel_id=1, source_target_pairs={{0,64},{8,456},{64,128},{72,8},{128,192},{136,72},{192,256},{200,1... | collective-permute-start | bytes 811016 | tf_op jit(solution)/shard_map/ppermute | solution.py:183
  57.9 13.8 %copy-start.5 = (bf16[2,528,128]{2,1,0:T(8,128)(2,1)}, bf16[2,528,128]{2,1,0:T(8,128)(2,1)S(1)}, u32[]{:S(2)}) copy-start(bf16[2,528,128]{2,1,0:T(8,128)(2,1)S(1)} %collective-permute-done.6.refs_7_) | copy-start | bytes 811012
  59.0 12.6 %collective-permute-start.8 = (bf16[3,2,528,128]{3,2,1,0:T(8,128)(2,1)S(1)}, bf16[3,2,528,128]{3,2,1,0:T(8,128)(2,1)S(1)}, u32[]{:S(2)}, u32[]{:S(2)}) collective-permute-start(bf16[3,2,528,128]{3,2,1,0:T(8,128)(2,1)S(1)} %pad_maximum_fusion), channel_id=1, source_target_pairs={{0,8},{8,0},{1,9},{9,1},{2,10},{10,2},{3,11},{11,3},{4,12},{12,4},... | collective-permute-start | bytes 2433032 | tf_op jit(solution)/shard_map/ppermute | solution.py:156
  64.1 7.5 %collective-permute-start.7 = (bf16[2,528,128]{2,1,0:T(8,128)(2,1)S(1)}, bf16[2,528,128]{2,1,0:T(8,128)(2,1)S(1)}, u32[]{:S(2)}, u32[]{:S(2)}) collective-permute-start(bf16[2,528,128]{2,1,0:T(8,128)(2,1)S(1)} %collective-permute-done.6.refs_7_), channel_id=1, source_target_pairs={{0,64},{8,456},{64,128},{72,8},{128,192},{136,72},{192,256},{200,1... | collective-permute-start | bytes 811016 | tf_op jit(solution)/shard_map/ppermute | solution.py:184
  71.6 0.7 copy-start.6
  71.6 1.0 copy-start.3
  71.7 1.3 copy-start.2
  82.7 17.4 %collective-permute-start.9 = (bf16[4,4,2,128,128]{4,3,2,1,0:T(8,128)(2,1)}, bf16[4,4,2,128,128]{4,3,2,1,0:T(8,128)(2,1)S(1)}, u32[]{:S(2)}, u32[]{:S(2)}) collective-permute-start(bf16[4,4,2,128,128]{4,3,2,1,0:T(8,128)(2,1)} %terms.3), channel_id=1, source_target_pairs={{0,1},{1,0},{2,3},{3,2},{4,5},{5,4},{6,7},{7,6},{8,15},{9,10},{10,... | collective-permute-start | bytes 3145736 | tf_op jit(solution)/shard_map/ppermute | solution.py:222
